TPU v7x, 32 devices: a whole 2x2x4 slice. The times are simulated.
32 devices in a mesh: tile: 32 (over z, y, x, core).
Axes of the slice: x: 2, y: 2, z: 4, core: 2. Of those that a mesh axis runs over, the one named last changes fastest.
Arguments:
- fields: float32 [64, 144, 800], P('tile'), may hold values from -6 to 6
- cotangent: float32 [64, 144, 800], P('tile'), may hold values from -6 to 6
- kernel: float32 [49, 800], replicated, may hold values from -0.875 to 0.875
- norm_gain: float32 [800], replicated, may hold values from 0.5 to 1.5
- norm_shift: float32 [800], replicated, may hold values from -3 to 3
- weight_in: bfloat16 [800, 3200], replicated, may hold values from -0.21875 to 0.21875
- bias_in: float32 [3200], replicated, may hold values from -3 to 3
- weight_out: bfloat16 [3200, 800], replicated, may hold values from -0.109375 to 0.109375
- bias_out: float32 [800], replicated, may hold values from -3 to 3
- neighbours: int32 [64, 8], P('tile'), may hold values from -1 to 63, as said below
- land_mask: int32 [64, 144], P('tile'), may hold values from 0 to 1, as said below
Outputs:
- block_out: float32 [64, 144, 800], P('tile')
- fields_grad: float32 [64, 144, 800], P('tile')
- kernel_grad: float32 [49, 800], replicated
- gain_grad: float32 [800], replicated
- shift_grad: float32 [800], replicated
- weight_in_grad: float32 [256, 10000], P('tile')
- bias_in_grad: float32 [3200], replicated
- weight_out_grad: float32 [256, 10000], P('tile')
- bias_out_grad: float32 [800], replicated
Inputs may be any that keep to these rules, and one draw needn't show every extreme that they name: `land_mask`: slots that hold an ocean tile come first on each device, and a slot holds one exactly where its row has a one (its cell 0 is then ocean). Each device holds 1 to 1 tiles, some device exactly 1; device i and device i + 16 together hold exactly 2. `neighbours`: an entry is the global slot (device times 2 plus slot) of the neighbouring ocean tile, or -1 for land, the grid's edge and empty slots. Ocean tiles run in grid order over devices and slots, so a neighbour lies at most 7 devices away, and in every draw some lie exactly that far.
All inputs are finite; a program needn't handle non-finite values.
Results may differ from a plain program's by a relative error of at most 0.0055.
Values may be sent and summed in bfloat16 or wider, within the bound.
A program may use at most 192 MiB of HBM per device.

v0:
```python
import jax
import jax.numpy as jnp
from jax import lax
from jax.sharding import PartitionSpec as P

TILE_SIDE = 12
KERNEL = 7
CELLS = 144
REACH = 7


EPSILON = 1e-05
SQRT_HALF = 0.7071067811865476
INV_ROOT_TAU = 0.3989422804014327


def from_behind(shard, axis, by):
    size = lax.axis_size(axis)
    pairs = [(i, i + by) for i in range(size) if 0 <= i + by < size]
    return lax.ppermute(shard, axis, pairs)


def gelu_value(pre):
    return 0.5 * pre * (1.0 + lax.erf(pre * SQRT_HALF))


def gelu_slope(pre):
    return 0.5 * (1.0 + lax.erf(pre * SQRT_HALF)) + pre * INV_ROOT_TAU * jnp.exp(-0.5 * pre * pre)


def pad_tiles(centre, nearby):
    margin = KERNEL // 2
    upper_rows = jnp.concatenate(
        [
            nearby[:, 0, -margin:, -margin:],
            nearby[:, 1, -margin:, :],
            nearby[:, 2, -margin:, :margin],
        ],
        axis=2,
    )
    middle = jnp.concatenate([nearby[:, 3, :, -margin:], centre, nearby[:, 4, :, :margin]], axis=2)
    bottom = jnp.concatenate(
        [nearby[:, 5, :margin, -margin:], nearby[:, 6, :margin, :], nearby[:, 7, :margin, :margin]],
        axis=2,
    )
    return jnp.concatenate([upper_rows, middle, bottom], axis=1)


def depthwise(centre, nearby, kernel):
    padded = pad_tiles(centre, nearby)
    tile_side = centre.shape[1]
    summed = jnp.zeros(centre.shape, jnp.float32)
    for row_tap in range(KERNEL):
        for col_tap in range(KERNEL):
            summed = (
                summed
                + kernel[row_tap * KERNEL + col_tap]
                * padded[:, row_tap : row_tap + tile_side, col_tap : col_tap + tile_side]
            )
    return summed


def feed_both(normed_low, grads_low, weight_in, bias_in, weight_out, bias_out):
    width = normed_low.shape[-1]
    rows = normed_low.reshape(-1, width)
    upstream = grads_low.reshape(-1, width)
    pre = jnp.dot(rows, weight_in, preferred_element_type=jnp.float32) + bias_in
    act_low = gelu_value(pre).astype(jnp.bfloat16)
    branch = jnp.dot(act_low, weight_out, preferred_element_type=jnp.float32) + bias_out
    act_grad = lax.dot_general(
        upstream, weight_out, (((1,), (1,)), ((), ())), preferred_element_type=jnp.float32
    )
    pre_low = (act_grad * gelu_slope(pre)).astype(jnp.bfloat16)
    normed_grad = lax.dot_general(
        pre_low, weight_in, (((1,), (1,)), ((), ())), preferred_element_type=jnp.float32
    )
    in_grad = lax.dot_general(
        rows, pre_low, (((0,), (0,)), ((), ())), preferred_element_type=jnp.float32
    )
    out_grad = lax.dot_general(
        act_low, upstream, (((0,), (0,)), ((), ())), preferred_element_type=jnp.float32
    )
    in_bias = jnp.sum(pre_low, axis=0, dtype=jnp.float32)
    out_bias = jnp.sum(upstream, axis=0, dtype=jnp.float32)
    return (
        branch.reshape(normed_low.shape),
        normed_grad.reshape(normed_low.shape),
        in_grad,
        in_bias,
        out_grad,
        out_bias,
    )


def local(
    fields,
    cotangent,
    kernel,
    norm_gain,
    norm_shift,
    weight_in,
    bias_in,
    weight_out,
    bias_out,
    neighbours,
    land_mask,
):
    position = lax.axis_index("tile")
    devices = lax.axis_size("tile")
    slots = fields.shape[0]
    width = fields.shape[-1]
    ocean = land_mask.astype(jnp.float32)
    cell_weight = ocean[:, :, None]
    arrivals = []
    for offset in range(-REACH, REACH + 1):
        if offset == 0:
            arrivals.append(fields)
        else:
            arrivals.append(from_behind(fields, "tile", -offset))
    stacked = jnp.concatenate(arrivals + [jnp.zeros((1,) + fields.shape[1:], jnp.float32)], axis=0)
    bucket = (2 * REACH + 1) * slots
    source = neighbours // slots - position + REACH
    places = jnp.where(neighbours < 0, bucket, source * slots + neighbours % slots).reshape(-1)
    nearby = jnp.take(stacked, places, axis=0).reshape(slots, 8, TILE_SIDE, TILE_SIDE, width)
    centre = fields.reshape(slots, TILE_SIDE, TILE_SIDE, width)
    conv_tiles, pullback = jax.vjp(depthwise, centre, nearby, kernel)
    conv = conv_tiles.reshape(fields.shape)
    ocean_count, first_sum = lax.psum(
        (jnp.sum(ocean), jnp.sum(conv * cell_weight, axis=(0, 1))), "tile"
    )
    centre_mean = first_sum / ocean_count
    spread = (
        lax.psum(jnp.sum(jnp.square(conv - centre_mean) * cell_weight, axis=(0, 1)), "tile")
        / ocean_count
    )
    inv_spread = lax.rsqrt(spread + EPSILON)
    scaled = (conv - centre_mean) * inv_spread
    normed_low = (scaled * norm_gain + norm_shift).astype(jnp.bfloat16)
    grads_low = (cotangent * cell_weight).astype(jnp.bfloat16)
    branch, normed_grad, in_grad, in_bias, out_grad, out_bias = feed_both(
        normed_low, grads_low, weight_in, bias_in, weight_out, bias_out
    )
    block_out = (fields + branch) * cell_weight
    grad_rows = 8 * devices
    weight_in_grad, weight_out_grad = (
        lax.psum_scatter(in_grad.reshape(grad_rows, -1), "tile", scatter_dimension=0, tiled=True),
        lax.psum_scatter(out_grad.reshape(grad_rows, -1), "tile", scatter_dimension=0, tiled=True),
    )
    shift_part = jnp.sum(normed_grad, axis=(0, 1))
    gain_part = jnp.sum(normed_grad * scaled, axis=(0, 1))
    shift_grad, gain_grad, bias_in_grad, bias_out_grad = lax.psum(
        (shift_part, gain_part, in_bias, out_bias), "tile"
    )
    conv_grad = (
        norm_gain
        * inv_spread
        * (normed_grad - cell_weight * (shift_grad + scaled * gain_grad) / ocean_count)
    )
    centre_grad, nearby_grad, kernel_part = pullback(conv_grad.reshape(centre.shape))
    choose = (places[None, :] == jnp.arange(bucket, dtype=jnp.int32)[:, None]).astype(jnp.float32)
    outgoing = jnp.dot(
        choose, nearby_grad.reshape(slots * 8, -1), precision=lax.Precision.HIGHEST
    ).reshape(2 * REACH + 1, slots, CELLS, width)
    fields_grad = cotangent * cell_weight + centre_grad.reshape(fields.shape) + outgoing[REACH]
    for offset in range(-REACH, REACH + 1):
        if offset != 0:
            fields_grad = fields_grad + from_behind(
                outgoing[offset + REACH].astype(jnp.bfloat16), "tile", offset
            ).astype(jnp.float32)
    kernel_grad = lax.psum(kernel_part, "tile")
    return (
        block_out,
        fields_grad,
        kernel_grad,
        gain_grad,
        shift_grad,
        weight_in_grad,
        bias_in_grad,
        weight_out_grad,
        bias_out_grad,
    )


def solution(mesh):
    return jax.shard_map(
        local,
        mesh=mesh,
        in_specs=(
            P("tile", None, None),
            P("tile", None, None),
            P(),
            P(),
            P(),
            P(),
            P(),
            P(),
            P(),
            P("tile", None),
            P("tile", None),
        ),
        out_specs=(
            P("tile", None, None),
            P("tile", None, None),
            P(),
            P(),
            P(),
            P("tile", None),
            P(),
            P("tile", None),
            P(),
        ),
        check_vma=False,
    )
```

profile of v0, /device:TPU:0, one launch (start us, length us, event | category | flops | bytes accessed | tf_op | source)
XLA Modules:
  0.0 1177.6 jit_solution(11335055005801507104)
XLA Ops:
  8.7 7.1 collective-permute-start.2
  45.4 60.7 %collective-permute-start.5 = (f32[2,144,800]{2,1,0:T(8,128)S(1)}, f32[2,144,800]{2,1,0:T(8,128)S(1)}, u32[]{:S(2)}, u32[]{:S(2)}) collective-permute-start(f32[2,144,800]{2,1,0:T(8,128)S(1)} %copy-done.4), channel_id=1, source_target_pairs={{0,2},{1,3},{2,4},{3,5},{4,6},{5,7},{6,8},{7,9},{8,10},{9,11},{10,... | collective-permute-start | bytes 2764808 | tf_op jit(solution)/shard_map/ppermute | solution.py:20
  136.4 11.9 %collective-permute-done.9 = f32[2,144,800]{2,1,0:T(8,128)S(1)} collective-permute-done((f32[2,144,800]{2,1,0:T(8,128)S(1)}, f32[2,144,800]{2,1,0:T(8,128)S(1)}, u32[]{:S(2)}, u32[]{:S(2)}) %collective-permute-start.9) | collective-permute-done | bytes 921632 | tf_op jit(solution)/shard_map/ppermute | solution.py:20
  149.3 73.5 %collective-permute-done.10 = f32[2,144,800]{2,1,0:T(8,128)S(1)} collective-permute-done((f32[2,144,800]{2,1,0:T(8,128)S(1)}, f32[2,144,800]{2,1,0:T(8,128)S(1)}, u32[]{:S(2)}, u32[]{:S(2)}) %collective-permute-start.10) | collective-permute-done | bytes 921632 | tf_op jit(solution)/shard_map/ppermute | solution.py:20
  230.8 9.9 gather_fusion
  249.9 13.0 %maximum_maximum_fusion = (f32[2,15,18,800]{3,0,2,1:T(2,128)S(1)}, f32[2,15,18,800]{3,0,2,1:T(2,128)S(1)}) fusion(f32[2,12,3,800]{3,0,2,1:T(2,128)S(1)} %get-tuple-element.231, f32[2,12,12,800]{3,0,2,1:T(2,128)S(1)} %bitcast.51, f32[2,12,3,800]{3,0,2,1:T(2,128)S(1)} %get-tuple-element.232, f32[2,3,3,800]{3,0,2,1:T(2,128)S(1)} %get-tuple-element.236, ...), kind=kLoop, calls=%fused_computation.14 | loop fusion | flops 4320000 | bytes 5529600 | tf_op jit(solution)/shard_map/jvp()/concatenate | solution.py:46
  263.2 35.1 %multiply_reduce_fusion.51 = (f32[800]{0:T(1024)}, f32[2,12,12,800]{3,0,2,1:T(2,128)S(1)}) fusion(f32[2,12,12]{0,2,1:T(8,128)S(1)} %copy-done.16, f32[2,15,18,800]{3,0,2,1:T(2,128)S(1)} %get-tuple-element.173, f32[800]{0:T(1024)S(1)} %copy-done.80, f32[800]{0:T(1024)S(1)} %get-tuple-element.123, f32[800]{0:T(1024)S(1)} %get-tuple-element.76, ...), kind=kLoop, calls=%fused_computation.103 | loop fusion | flops 24191200 | bytes 41172352 | tf_op jit(solution)/shard_map/reduce_sum | solution.py:129
  299.6 98.0 %all-reduce.109 = (f32[800]{0:T(1024)S(1)}, f32[]{:T(128)}) all-reduce(f32[800]{0:T(1024)S(1)} %copy-done.97, f32[]{:T(128)} %convert_reduce_fusion.2), channel_id=1, replica_groups=mesh['tile'=32] {'tile'}, use_global_device_ids=true, to_apply=%region_1.2 | all-reduce | flops 801 | bytes 6408 | tf_op jit(solution)/shard_map/psum | solution.py:128
  400.0 40.3 %psum.58 = f32[800]{0:T(1024)} all-reduce(f32[800]{0:T(1024)S(1)} %multiply_reduce_fusion.50), channel_id=1, replica_groups=mesh['tile'=32] {'tile'}, use_global_device_ids=true, to_apply=%region_5.6 | all-reduce | flops 800 | bytes 6400 | tf_op jit(solution)/shard_map/psum | solution.py:133
  456.4 6.2 convert_reduce_fusion
  468.8 41.5 %all-reduce.108 = (f32[800]{0:T(1024)}, f32[800]{0:T(1024)}, f32[3200]{0:T(1024)}, f32[800]{0:T(1024)}) all-reduce(f32[800]{0:T(1024)} %get-tuple-element.74, f32[800]{0:T(1024)} %get-tuple-element.73, f32[3200]{0:T(1024)} %get-tuple-element.227, f32[800]{0:T(1024)} %get-tuple-element.136), channel_id=1, replica_groups=mesh['tile'=32] {'tile'}, use_global_device_ids=true, to_apply=%region_9.10 | all-reduce | flops 5600 | bytes 44800 | tf_op jit(solution)/shard_map/psum | solution.py:151
  510.4 15.7 %multiply_reduce_fusion.48 = (f32[800]{0:T(1024)S(1)}, f32[800]{0:T(1024)S(1)}, f32[800]{0:T(1024)S(1)}, f32[800]{0:T(1024)S(1)}, f32[800]{0:T(1024)S(1)}, /*ind...) fusion(f32[2,15,18,800]{3,0,2,1:T(2,128)} %copy-done, ...), kind=kLoop, calls=%fused_computation.97 | loop fusion | flops 10123200 | bytes 19428356 | tf_op jit(solution)/shard_map/transpose(jvp())/reduce_sum | solution.py:57
  526.2 9.1 multiply_reduce_fusion.20
  535.4 7.5 multiply_reduce_fusion.27
  543.0 6.7 fusion.26
  549.9 8.2 multiply_reduce_fusion.47
  558.1 6.2 fusion.39
  570.5 8.5 broadcast_multiply_fusion
  579.0 75.2 %pad_add_fusion.1 = f32[2,18,18,800]{3,0,2,1:T(2,128)S(1)} fusion(f32[2,12,12,800]{3,0,2,1:T(2,128)} %get-tuple-element.174, f32[2,12,12,800]{3,0,2,1:T(2,128)} %get-tuple-element.175, f32[2,12,12,800]{3,0,2,1:T(2,128)} %get-tuple-element.176, f32[2,12,12,800]{3,0,2,1:T(2,128)} %get-tuple-element.177, f32[2,12,12,800]{3,0,2,1:T(2,128)} %get-tuple-element.178, ...), kind=kLoop, calls=%fused_computation.13 | loop fusion | flops 24883200 | bytes 47232000 | tf_op jit(solution)/shard_map/transpose(jvp())/add_any | solution.py:58
  680.5 12.1 %reshape.406 = f32[256,10000]{1,0:T(8,128)} reshape(f32[800,3200]{1,0:T(8,128)} %fusion.26) | data formatting | bytes 20480000 | tf_op jit(solution)/shard_map/reshape | solution.py:146
  699.6 14.0 %reshape.407 = f32[256,10000]{1,0:T(8,128)} reshape(f32[3200,800]{1,0:T(8,128)} %fusion.39) | data formatting | bytes 20480000 | tf_op jit(solution)/shard_map/reshape | solution.py:147
  724.5 13.9 %reshape.405 = f32[16,115200]{1,0:T(8,128)} reshape(f32[2,8,12,12,800]{4,3,2,1,0:T(8,128)} %copy.69) | data formatting | bytes 14745600 | tf_op jit(solution)/shard_map/reshape | solution.py:162
  738.8 14.8 %fusion.38 = (bf16[30,115200]{1,0:T(8,128)(2,1)}, f32[30,115200]{1,0:T(8,128)}) fusion(f32[16,115200]{1,0:T(8,128)} %reshape.405, s32[16]{0:T(128)} %reshape.404), kind=kOutput, calls=%fused_computation.265 | convolution fusion | flops 667008512 | bytes 28108864 | tf_op jit(solution)/shard_map/dot_general | solution.py:161
  755.8 15.9 %fusion.37 = (bf16[2,115200]{1,0:T(2,128)(2,1)}, bf16[2,115200]{1,0:T(2,128)(2,1)}, bf16[2,115200]{1,0:T(2,128)(2,1)}, bf16[2,115200]{1,0:T(2,128)(2,1)S(1)}, bf...) fusion(bf16[30,115200]{1,0:T(8,128)(2,1)} %get-tuple-element.229), kind=kLoop, calls=%fused_computation.264 | loop fusion | bytes 12902400 | tf_op jit(solution)/shard_map/slice | solution.py:168
  804.0 12.1 %collective-permute-done.16 = bf16[2,144,800]{2,1,0:T(8,128)(2,1)} collective-permute-done((bf16[2,144,800]{2,1,0:T(8,128)(2,1)}, bf16[2,144,800]{2,1,0:T(8,128)(2,1)}, u32[]{:S(2)}, u32[]{:S(2)}) %collective-permute-start.16) | collective-permute-done | bytes 460832 | tf_op jit(solution)/shard_map/ppermute | solution.py:20
  818.2 16.6 %collective-permute-start.22 = (bf16[2,144,800]{2,1,0:T(8,128)(2,1)}, bf16[2,144,800]{2,1,0:T(8,128)(2,1)}, u32[]{:S(2)}, u32[]{:S(2)}) collective-permute-start(bf16[2,144,800]{2,1,0:T(8,128)(2,1)} %convert_element_type.143), channel_id=1, source_target_pairs={{0,2},{1,3},{2,4},{3,5},{4,6},{5,7},{6,8},{7,9},{8,10},{9,11},{10,... | collective-permute-start | bytes 1382408 | tf_op jit(solution)/shard_map/ppermute | solution.py:20
  834.9 21.6 %collective-permute-start.23 = (bf16[2,144,800]{2,1,0:T(8,128)(2,1)}, bf16[2,144,800]{2,1,0:T(8,128)(2,1)}, u32[]{:S(2)}, u32[]{:S(2)}) collective-permute-start(bf16[2,144,800]{2,1,0:T(8,128)(2,1)} %convert_element_type.145), channel_id=1, source_target_pairs={{0,3},{1,4},{2,5},{3,6},{4,7},{5,8},{6,9},{7,10},{8,11},{9,12},{10... | collective-permute-start | bytes 1382408 | tf_op jit(solution)/shard_map/ppermute | solution.py:20
  867.5 18.3 %collective-permute-start.24 = (bf16[2,144,800]{2,1,0:T(8,128)(2,1)}, bf16[2,144,800]{2,1,0:T(8,128)(2,1)}, u32[]{:S(2)}, u32[]{:S(2)}) collective-permute-start(bf16[2,144,800]{2,1,0:T(8,128)(2,1)} %convert_element_type.147), channel_id=1, source_target_pairs={{0,4},{1,5},{2,6},{3,7},{4,8},{5,9},{6,10},{7,11},{8,12},{9,13},{1... | collective-permute-start | bytes 1382408 | tf_op jit(solution)/shard_map/ppermute | solution.py:20
  885.8 12.8 %collective-permute-start.25 = (bf16[2,144,800]{2,1,0:T(8,128)(2,1)}, bf16[2,144,800]{2,1,0:T(8,128)(2,1)}, u32[]{:S(2)}, u32[]{:S(2)}) collective-permute-start(bf16[2,144,800]{2,1,0:T(8,128)(2,1)} %convert_element_type.149), channel_id=1, source_target_pairs={{0,5},{1,6},{2,7},{3,8},{4,9},{5,10},{6,11},{7,12},{8,13},{9,14},{... | collective-permute-start | bytes 1382408 | tf_op jit(solution)/shard_map/ppermute | solution.py:20
  903.8 16.1 %collective-permute-start.27 = (bf16[2,144,800]{2,1,0:T(8,128)(2,1)}, bf16[2,144,800]{2,1,0:T(8,128)(2,1)}, u32[]{:S(2)}, u32[]{:S(2)}) collective-permute-start(bf16[2,144,800]{2,1,0:T(8,128)(2,1)} %convert_element_type.153), channel_id=1, source_target_pairs={{0,7},{1,8},{2,9},{3,10},{4,11},{5,12},{6,13},{7,14},{8,15},{9,16}... | collective-permute-start | bytes 1382408 | tf_op jit(solution)/shard_map/ppermute | solution.py:20
  932.2 6.2 fusion.22
  938.4 227.1 %all-reduce.113.cloned.1.call-done = (f32[49,800]{1,0:T(8,128)}, f32[256,10000]{1,0:T(8,128)}, f32[256,10000]{1,0:T(8,128)}) async-done(((f32[49,800]{1,0:T(8,128)}, f32[256,10000]{1,0:T(8,128)}, f32[256,10000]{1,0:T(8,128)}), (f32[49,800]{1,0:T(8,128)}, f32[256,10000]{1,0:T(8,128)}, f32[256,10000]{1,0:T(8,128)})) %all-reduce.113.cloned.1.call-update) | async-done | bytes 20636816 | tf_op jit(solution)/shard_map/psum | solution.py:170
  (457 shorter events, 225.0 us)
Async XLA Ops:
  7.2 1158.3 %all-reduce.113.cloned.1.call-start = ((), (), s32[]{:S(2)}) async-start(), calls=%async_computation | async-start | bytes 41820160 | tf_op jit(solution)/shard_map/psum | solution.py:170
  7.2 28.0 %collective-permute-start.8 = (f32[2,144,800]{2,1,0:T(8,128)}, f32[2,144,800]{2,1,0:T(8,128)S(1)}, u32[]{:S(2)}, u32[]{:S(2)}) collective-permute-start(f32[2,144,800]{2,1,0:T(8,128)} %param.11), channel_id=1, source_target_pairs={{2,0},{3,1},{4,2},{5,3},{6,4},{7,5},{8,6},{9,7},{10,8},{11,9},{12,... | collective-permute-start | bytes 2764808 | tf_op jit(solution)/shard_map/ppermute | solution.py:20
  8.7 36.7 %collective-permute-start.2 = (f32[2,144,800]{2,1,0:T(8,128)}, f32[2,144,800]{2,1,0:T(8,128)}, u32[]{:S(2)}, u32[]{:S(2)}) collective-permute-start(f32[2,144,800]{2,1,0:T(8,128)} %param.11), channel_id=1, source_target_pairs={{0,5},{1,6},{2,7},{3,8},{4,9},{5,10},{6,11},{7,12},{8,13},{9,14},{... | collective-permute-start | bytes 2764808 | tf_op jit(solution)/shard_map/ppermute | solution.py:20
  15.8 100.6 %collective-permute-start.3 = (f32[2,144,800]{2,1,0:T(8,128)}, f32[2,144,800]{2,1,0:T(8,128)}, u32[]{:S(2)}, u32[]{:S(2)}) collective-permute-start(f32[2,144,800]{2,1,0:T(8,128)} %param.11), channel_id=1, source_target_pairs={{0,4},{1,5},{2,6},{3,7},{4,8},{5,9},{6,10},{7,11},{8,12},{9,13},{1... | collective-permute-start | bytes 2764808 | tf_op jit(solution)/shard_map/ppermute | solution.py:20
  21.0 85.8 %collective-permute-start.1 = (f32[2,144,800]{2,1,0:T(8,128)}, f32[2,144,800]{2,1,0:T(8,128)}, u32[]{:S(2)}, u32[]{:S(2)}) collective-permute-start(f32[2,144,800]{2,1,0:T(8,128)} %param.11), channel_id=1, source_target_pairs={{0,6},{1,7},{2,8},{3,9},{4,10},{5,11},{6,12},{7,13},{8,14},{9,15},... | collective-permute-start | bytes 2764808 | tf_op jit(solution)/shard_map/ppermute | solution.py:20
  23.3 84.9 %collective-permute-start = (f32[2,144,800]{2,1,0:T(8,128)}, f32[2,144,800]{2,1,0:T(8,128)}, u32[]{:S(2)}, u32[]{:S(2)}) collective-permute-start(f32[2,144,800]{2,1,0:T(8,128)} %param.11), channel_id=1, source_target_pairs={{0,7},{1,8},{2,9},{3,10},{4,11},{5,12},{6,13},{7,14},{8,15},{9,16}... | collective-permute-start | bytes 2764808 | tf_op jit(solution)/shard_map/ppermute | solution.py:20
  30.0 232.9 %copy-start.22 = (f32[800]{0:T(1024)}, f32[800]{0:T(1024)S(1)}, u32[]{:S(2)}) copy-start(f32[800]{0:T(1024)S(1)} %get-tuple-element.94) | copy-start | bytes 9604
  35.2 84.6 %collective-permute-start.4 = (f32[2,144,800]{2,1,0:T(8,128)}, f32[2,144,800]{2,1,0:T(8,128)}, u32[]{:S(2)}, u32[]{:S(2)}) collective-permute-start(f32[2,144,800]{2,1,0:T(8,128)} %param.11), channel_id=1, source_target_pairs={{0,3},{1,4},{2,5},{3,6},{4,7},{5,8},{6,9},{7,10},{8,11},{9,12},{10... | collective-permute-start | bytes 2764808 | tf_op jit(solution)/shard_map/ppermute | solution.py:20
  43.6 205.9 %copy-start.2 = (f32[2,144,800]{2,0,1:T(2,128)}, f32[2,144,800]{2,0,1:T(2,128)S(1)}, u32[]{:S(2)}) copy-start(f32[2,144,800]{2,0,1:T(2,128)S(1)} %copy.63) | copy-start | bytes 2764804
  45.4 217.5 %copy-start.24 = (f32[800]{0:T(1024)}, f32[800]{0:T(1024)S(1)}, u32[]{:S(2)}) copy-start(f32[800]{0:T(1024)S(1)} %get-tuple-element.75) | copy-start | bytes 9604
  45.4 81.7 %collective-permute-start.5 = (f32[2,144,800]{2,1,0:T(8,128)S(1)}, f32[2,144,800]{2,1,0:T(8,128)S(1)}, u32[]{:S(2)}, u32[]{:S(2)}) collective-permute-start(f32[2,144,800]{2,1,0:T(8,128)S(1)} %copy-done.4), channel_id=1, source_target_pairs={{0,2},{1,3},{2,4},{3,5},{4,6},{5,7},{6,8},{7,9},{8,10},{9,11},{10,... | collective-permute-start | bytes 2764808 | tf_op jit(solution)/shard_map/ppermute | solution.py:20
  106.8 22.6 %collective-permute-start.6 = (f32[2,144,800]{2,1,0:T(8,128)S(1)}, f32[2,144,800]{2,1,0:T(8,128)S(1)}, u32[]{:S(2)}, u32[]{:S(2)}) collective-permute-start(f32[2,144,800]{2,1,0:T(8,128)S(1)} %copy-done.4), channel_id=1, source_target_pairs={{0,1},{1,2},{2,3},{3,4},{4,5},{5,6},{6,7},{7,8},{8,9},{9,10},{10,1... | collective-permute-start | bytes 2764808 | tf_op jit(solution)/shard_map/ppermute | solution.py:20
  108.2 23.6 %collective-permute-start.7 = (f32[2,144,800]{2,1,0:T(8,128)S(1)}, f32[2,144,800]{2,1,0:T(8,128)S(1)}, u32[]{:S(2)}, u32[]{:S(2)}) collective-permute-start(f32[2,144,800]{2,1,0:T(8,128)S(1)} %copy-done.4), channel_id=1, source_target_pairs={{1,0},{2,1},{3,2},{4,3},{5,4},{6,5},{7,6},{8,7},{9,8},{10,9},{11,1... | collective-permute-start | bytes 2764808 | tf_op jit(solution)/shard_map/ppermute | solution.py:20
  116.3 31.9 %collective-permute-start.9 = (f32[2,144,800]{2,1,0:T(8,128)S(1)}, f32[2,144,800]{2,1,0:T(8,128)S(1)}, u32[]{:S(2)}, u32[]{:S(2)}) collective-permute-start(f32[2,144,800]{2,1,0:T(8,128)S(1)} %copy-done.4), channel_id=1, source_target_pairs={{3,0},{4,1},{5,2},{6,3},{7,4},{8,5},{9,6},{10,7},{11,8},{12,9},{13... | collective-permute-start | bytes 2764808 | tf_op jit(solution)/shard_map/ppermute | solution.py:20
  119.9 102.9 %collective-permute-start.10 = (f32[2,144,800]{2,1,0:T(8,128)S(1)}, f32[2,144,800]{2,1,0:T(8,128)S(1)}, u32[]{:S(2)}, u32[]{:S(2)}) collective-permute-start(f32[2,144,800]{2,1,0:T(8,128)S(1)} %copy-done.4), channel_id=1, source_target_pairs={{4,0},{5,1},{6,2},{7,3},{8,4},{9,5},{10,6},{11,7},{12,8},{13,9},{1... | collective-permute-start | bytes 2764808 | tf_op jit(solution)/shard_map/ppermute | solution.py:20
  127.1 99.7 %collective-permute-start.11 = (f32[2,144,800]{2,1,0:T(8,128)S(1)}, f32[2,144,800]{2,1,0:T(8,128)S(1)}, u32[]{:S(2)}, u32[]{:S(2)}) collective-permute-start(f32[2,144,800]{2,1,0:T(8,128)S(1)} %copy-done.4), channel_id=1, source_target_pairs={{5,0},{6,1},{7,2},{8,3},{9,4},{10,5},{11,6},{12,7},{13,8},{14,9},{... | collective-permute-start | bytes 2764808 | tf_op jit(solution)/shard_map/ppermute | solution.py:20
  129.5 98.4 %collective-permute-start.12 = (f32[2,144,800]{2,1,0:T(8,128)S(1)}, f32[2,144,800]{2,1,0:T(8,128)S(1)}, u32[]{:S(2)}, u32[]{:S(2)}) collective-permute-start(f32[2,144,800]{2,1,0:T(8,128)S(1)} %copy-done.4), channel_id=1, source_target_pairs={{6,0},{7,1},{8,2},{9,3},{10,4},{11,5},{12,6},{13,7},{14,8},{15,9},... | collective-permute-start | bytes 2764808 | tf_op jit(solution)/shard_map/ppermute | solution.py:20
  131.8 97.1 %collective-permute-start.13 = (f32[2,144,800]{2,1,0:T(8,128)S(1)}, f32[2,144,800]{2,1,0:T(8,128)S(1)}, u32[]{:S(2)}, u32[]{:S(2)}) collective-permute-start(f32[2,144,800]{2,1,0:T(8,128)S(1)} %copy-done.4), channel_id=1, source_target_pairs={{7,0},{8,1},{9,2},{10,3},{11,4},{12,5},{13,6},{14,7},{15,8},{16,9}... | collective-permute-start | bytes 2764808 | tf_op jit(solution)/shard_map/ppermute | solution.py:20
  776.9 25.8 %collective-permute-start.15 = (bf16[2,144,800]{2,1,0:T(8,128)(2,1)}, bf16[2,144,800]{2,1,0:T(8,128)(2,1)}, u32[]{:S(2)}, u32[]{:S(2)}) collective-permute-start(bf16[2,144,800]{2,1,0:T(8,128)(2,1)} %convert_element_type.129), channel_id=1, source_target_pairs={{6,0},{7,1},{8,2},{9,3},{10,4},{11,5},{12,6},{13,7},{14,8},{15,9},... | collective-permute-start | bytes 1382408 | tf_op jit(solution)/shard_map/ppermute | solution.py:20
  780.8 35.3 %collective-permute-start.16 = (bf16[2,144,800]{2,1,0:T(8,128)(2,1)}, bf16[2,144,800]{2,1,0:T(8,128)(2,1)}, u32[]{:S(2)}, u32[]{:S(2)}) collective-permute-start(bf16[2,144,800]{2,1,0:T(8,128)(2,1)} %convert_element_type.131), channel_id=1, source_target_pairs={{5,0},{6,1},{7,2},{8,3},{9,4},{10,5},{11,6},{12,7},{13,8},{14,9},{... | collective-permute-start | bytes 1382408 | tf_op jit(solution)/shard_map/ppermute | solution.py:20
  782.1 36.1 %collective-permute-start.17 = (bf16[2,144,800]{2,1,0:T(8,128)(2,1)}, bf16[2,144,800]{2,1,0:T(8,128)(2,1)}, u32[]{:S(2)}, u32[]{:S(2)}) collective-permute-start(bf16[2,144,800]{2,1,0:T(8,128)(2,1)} %convert_element_type.133), channel_id=1, source_target_pairs={{4,0},{5,1},{6,2},{7,3},{8,4},{9,5},{10,6},{11,7},{12,8},{13,9},{1... | collective-permute-start | bytes 1382408 | tf_op jit(solution)/shard_map/ppermute | solution.py:20
  786.0 48.9 %collective-permute-start.18 = (bf16[2,144,800]{2,1,0:T(8,128)(2,1)}, bf16[2,144,800]{2,1,0:T(8,128)(2,1)}, u32[]{:S(2)}, u32[]{:S(2)}) collective-permute-start(bf16[2,144,800]{2,1,0:T(8,128)(2,1)} %convert_element_type.135), channel_id=1, source_target_pairs={{3,0},{4,1},{5,2},{6,3},{7,4},{8,5},{9,6},{10,7},{11,8},{12,9},{13... | collective-permute-start | bytes 1382408 | tf_op jit(solution)/shard_map/ppermute | solution.py:20
  800.3 67.2 %collective-permute-start.19 = (bf16[2,144,800]{2,1,0:T(8,128)(2,1)}, bf16[2,144,800]{2,1,0:T(8,128)(2,1)}, u32[]{:S(2)}, u32[]{:S(2)}) collective-permute-start(bf16[2,144,800]{2,1,0:T(8,128)(2,1)} %convert_element_type.137), channel_id=1, source_target_pairs={{2,0},{3,1},{4,2},{5,3},{6,4},{7,5},{8,6},{9,7},{10,8},{11,9},{12,... | collective-permute-start | bytes 1382408 | tf_op jit(solution)/shard_map/ppermute | solution.py:20
  802.7 83.1 %collective-permute-start.20 = (bf16[2,144,800]{2,1,0:T(8,128)(2,1)}, bf16[2,144,800]{2,1,0:T(8,128)(2,1)}, u32[]{:S(2)}, u32[]{:S(2)}) collective-permute-start(bf16[2,144,800]{2,1,0:T(8,128)(2,1)} %convert_element_type.139), channel_id=1, source_target_pairs={{1,0},{2,1},{3,2},{4,3},{5,4},{6,5},{7,6},{8,7},{9,8},{10,9},{11,1... | collective-permute-start | bytes 1382408 | tf_op jit(solution)/shard_map/ppermute | solution.py:20
  816.1 82.5 %collective-permute-start.21 = (bf16[2,144,800]{2,1,0:T(8,128)(2,1)}, bf16[2,144,800]{2,1,0:T(8,128)(2,1)}, u32[]{:S(2)}, u32[]{:S(2)}) collective-permute-start(bf16[2,144,800]{2,1,0:T(8,128)(2,1)} %convert_element_type.141), channel_id=1, source_target_pairs={{0,1},{1,2},{2,3},{3,4},{4,5},{5,6},{6,7},{7,8},{8,9},{9,10},{10,1... | collective-permute-start | bytes 1382408 | tf_op jit(solution)/shard_map/ppermute | solution.py:20
  818.2 85.5 %collective-permute-start.22 = (bf16[2,144,800]{2,1,0:T(8,128)(2,1)}, bf16[2,144,800]{2,1,0:T(8,128)(2,1)}, u32[]{:S(2)}, u32[]{:S(2)}) collective-permute-start(bf16[2,144,800]{2,1,0:T(8,128)(2,1)} %convert_element_type.143), channel_id=1, source_target_pairs={{0,2},{1,3},{2,4},{3,5},{4,6},{5,7},{6,8},{7,9},{8,10},{9,11},{10,... | collective-permute-start | bytes 1382408 | tf_op jit(solution)/shard_map/ppermute | solution.py:20
  834.9 85.0 %collective-permute-start.23 = (bf16[2,144,800]{2,1,0:T(8,128)(2,1)}, bf16[2,144,800]{2,1,0:T(8,128)(2,1)}, u32[]{:S(2)}, u32[]{:S(2)}) collective-permute-start(bf16[2,144,800]{2,1,0:T(8,128)(2,1)} %convert_element_type.145), channel_id=1, source_target_pairs={{0,3},{1,4},{2,5},{3,6},{4,7},{5,8},{6,9},{7,10},{8,11},{9,12},{10... | collective-permute-start | bytes 1382408 | tf_op jit(solution)/shard_map/ppermute | solution.py:20
  867.5 59.8 %collective-permute-start.24 = (bf16[2,144,800]{2,1,0:T(8,128)(2,1)}, bf16[2,144,800]{2,1,0:T(8,128)(2,1)}, u32[]{:S(2)}, u32[]{:S(2)}) collective-permute-start(bf16[2,144,800]{2,1,0:T(8,128)(2,1)} %convert_element_type.147), channel_id=1, source_target_pairs={{0,4},{1,5},{2,6},{3,7},{4,8},{5,9},{6,10},{7,11},{8,12},{9,13},{1... | collective-permute-start | bytes 1382408 | tf_op jit(solution)/shard_map/ppermute | solution.py:20
  885.8 41.5 %collective-permute-start.25 = (bf16[2,144,800]{2,1,0:T(8,128)(2,1)}, bf16[2,144,800]{2,1,0:T(8,128)(2,1)}, u32[]{:S(2)}, u32[]{:S(2)}) collective-permute-start(bf16[2,144,800]{2,1,0:T(8,128)(2,1)} %convert_element_type.149), channel_id=1, source_target_pairs={{0,5},{1,6},{2,7},{3,8},{4,9},{5,10},{6,11},{7,12},{8,13},{9,14},{... | collective-permute-start | bytes 1382408 | tf_op jit(solution)/shard_map/ppermute | solution.py:20
  898.6 28.7 %collective-permute-start.26 = (bf16[2,144,800]{2,1,0:T(8,128)(2,1)}, bf16[2,144,800]{2,1,0:T(8,128)(2,1)}, u32[]{:S(2)}, u32[]{:S(2)}) collective-permute-start(bf16[2,144,800]{2,1,0:T(8,128)(2,1)} %convert_element_type.151), channel_id=1, source_target_pairs={{0,6},{1,7},{2,8},{3,9},{4,10},{5,11},{6,12},{7,13},{8,14},{9,15},... | collective-permute-start | bytes 1382408 | tf_op jit(solution)/shard_map/ppermute | solution.py:20
  903.8 28.4 %collective-permute-start.27 = (bf16[2,144,800]{2,1,0:T(8,128)(2,1)}, bf16[2,144,800]{2,1,0:T(8,128)(2,1)}, u32[]{:S(2)}, u32[]{:S(2)}) collective-permute-start(bf16[2,144,800]{2,1,0:T(8,128)(2,1)} %convert_element_type.153), channel_id=1, source_target_pairs={{0,7},{1,8},{2,9},{3,10},{4,11},{5,12},{6,13},{7,14},{8,15},{9,16}... | collective-permute-start | bytes 1382408 | tf_op jit(solution)/shard_map/ppermute | solution.py:20
  919.9 12.3 %collective-permute-start.14 = (bf16[2,144,800]{2,1,0:T(8,128)(2,1)}, bf16[2,144,800]{2,1,0:T(8,128)(2,1)}, u32[]{:S(2)}, u32[]{:S(2)}) collective-permute-start(bf16[2,144,800]{2,1,0:T(8,128)(2,1)} %convert_element_type.127), channel_id=1, source_target_pairs={{7,0},{8,1},{9,2},{10,3},{11,4},{12,5},{13,6},{14,7},{15,8},{16,9}... | collective-permute-start | bytes 1382408 | tf_op jit(solution)/shard_map/ppermute | solution.py:20
  (139 other events, 2228.7 us)
Sparse Core Ops, SparseCore 0:
  755.9 409.5 all-reduce.112
where the time goes:
time: 1190 us; the launch traced here: 1180 us
  waiting for transfers between devices  342 us (29%)
  other arithmetic  202 us (17%)
  starting transfers between devices  195 us (16%)
  local copies, waits for them, and re-layouts  194 us (16%)
  blocking collectives  180 us (15%)
  matrix products  47.6 us (4%)
  between operations  16.5 us (1%)
    psum x1, waiting for transfers between devices, local(): kernel_grad = lax.psum(kernel_part, 'tile')  227 us
    ppermute x28, starting transfers between devices, from_behind(): return lax.ppermute(shard, axis, pairs)  195 us
    ppermute x28, waiting for transfers between devices, from_behind(): return lax.ppermute(shard, axis, pairs)  115 us
    psum x1, blocking collectives, local(): lax.psum((jnp.sum(ocean), jnp.sum(conv * cell_weight, axis=(0, 1))), 'tile')  98 us
    add_any x1, other arithmetic, depthwise(): padded[:, row_tap:row_tap + tile_side, col_tap:col_tap + tile_side]  75.2 us
    psum x1, blocking collectives, local(): lax.psum((shift_part, gain_part, in_bias, out_bias), 'tile')  41.5 us
    reduce_sum x4, other arithmetic, depthwise(): kernel[row_tap * KERNEL + col_tap]  40.5 us
    psum x1, blocking collectives, local(): lax.psum(jnp.sum(jnp.square(conv - centre_mean) * cell_weight, axis=(0, 1...  40.3 us
  transfers between devices with their start and end apart: 29, of which 9 were waited for; matrix products, arithmetic and copies ran while one was open for 8% of the time, Pallas kernels for 0%

commit v1 on v0

--- a/solution.py
+++ b/solution.py
@@ -1,17 +1,815 @@
+import functools
+import math
+
 import jax
 import jax.numpy as jnp
 from jax import lax
+from jax.experimental import pallas as pl
+from jax.experimental.pallas import tpu as pltpu
 from jax.sharding import PartitionSpec as P
 
 TILE_SIDE = 12
 KERNEL = 7
 CELLS = 144
 REACH = 7
-
+MARGIN = KERNEL // 2
+PAD_SIDE = TILE_SIDE + 2 * MARGIN
+EDGE = MARGIN * TILE_SIDE
+INNER = 8
+LANES = 128
+SUB = 8
 
 EPSILON = 1e-05
 SQRT_HALF = 0.7071067811865476
 INV_ROOT_TAU = 0.3989422804014327
+BF = jnp.bfloat16
+F32 = jnp.float32
+MESH = pl.DeviceIdType.MESH
+NN = (((1,), (0,)), ((), ()))
+NT = (((1,), (1,)), ((), ()))
+
+
+def dot(a, b, dims=NN, precision=None):
+    return lax.dot_general(a, b, dims, preferred_element_type=F32, precision=precision)
+
+
+def window(start, need, total):
+    width = min(total, (-(-(need + LANES - 1) // LANES)) * LANES)
+    first = jnp.minimum((start // LANES) * LANES, total - width)
+    return first, width
+
+
+def step_kernel(
+    N,
+    C,
+    H,
+    fields_hbm,
+    cot_hbm,
+    kernel_ref,
+    gain_ref,
+    shift_ref,
+    win_hbm,
+    bin_ref,
+    wout_hbm,
+    bout_ref,
+    nbr_ref,
+    mask_ref,
+    maskv_ref,
+    o_block,
+    o_fgrad,
+    o_kgrad,
+    o_vec,
+    o_win,
+    o_wout,
+    x_nat,
+    cot_nat,
+    win,
+    wout,
+    xc,
+    pad,
+    conv,
+    ngc,
+    kc,
+    gc,
+    strip_top,
+    strip_bot,
+    strip_lef,
+    strip_rig,
+    from_low,
+    from_high,
+    from_w,
+    from_e,
+    stat_a,
+    stat_b,
+    stat_sa,
+    stat_sb,
+    nrm,
+    ups,
+    actg,
+    branch,
+    nall,
+    uall,
+    wi_t,
+    wo_t,
+    bi_t,
+    act_t,
+    pg_t,
+    og,
+    ig,
+    zo_src,
+    zi_src,
+    zo_dst,
+    zi_dst,
+    tr,
+    tr_src,
+    tr_dst,
+    kg,
+    kg_slot,
+    kg_col,
+    kg_tot,
+    load_sem,
+    halo_send,
+    halo_recv,
+    vec_send,
+    vec_recv,
+    col_send,
+    col_recv,
+    rows_send,
+    rows_recv,
+    z_send,
+    z_recv,
+    tr_send,
+    tr_recv,
+    ks_send,
+    ks_recv,
+):
+    Q = N // INNER
+    hb = H // N
+    cb = C // N
+    LT = -(-C // LANES)
+    tail = C - (LT - 1) * LANES
+    me = lax.axis_index("tile")
+    p = lax.rem(me, INNER)
+    q = me // INNER
+
+    def remote(src, dst, ssem, rsem, dev):
+        return pltpu.make_async_remote_copy(
+            src_ref=src, dst_ref=dst, send_sem=ssem, recv_sem=rsem, device_id=(dev,), device_id_type=MESH
+        )
+
+    def in_plane(s):
+        return q * INNER + lax.rem(p + s, INNER)
+
+    def in_column(t):
+        return lax.rem(q + t, Q) * INNER + p
+
+    loads = [
+        pltpu.make_async_copy(fields_hbm.at[0], x_nat, load_sem.at[0]),
+        pltpu.make_async_copy(cot_hbm.at[0], cot_nat, load_sem.at[1]),
+        pltpu.make_async_copy(wout_hbm, wout, load_sem.at[2]),
+        pltpu.make_async_copy(win_hbm, win, load_sem.at[3]),
+    ]
+    for copy in loads:
+        copy.start()
+    barrier = pltpu.get_barrier_semaphore()
+
+    @pl.loop(1, REACH + 1)
+    def _(k):
+        @pl.when(me + k < N)
+        def _():
+            pl.semaphore_signal(barrier, inc=1, device_id=(me + k,), device_id_type=MESH)
+
+        @pl.when(me - k >= 0)
+        def _():
+            pl.semaphore_signal(barrier, inc=1, device_id=(me - k,), device_id_type=MESH)
+
+    @pl.loop(1, Q)
+    def _(t):
+        pl.semaphore_signal(barrier, inc=1, device_id=(in_column(t),), device_id_type=MESH)
+
+    def cells_from(dst, tile_of, count):
+        for t in range(SUB):
+            if t < LT:
+                v = tile_of(t)
+                if t == LT - 1 and tail < LANES:
+                    v = jnp.concatenate([v, jnp.zeros((count, LANES - tail), F32)], axis=1)
+            else:
+                v = jnp.zeros((count, LANES), F32)
+            dst[pl.ds(t, count, stride=SUB), :] = v
+
+    def lanes(t):
+        return slice(t * LANES, min((t + 1) * LANES, C))
+
+    cells_from(kc, lambda t: kernel_ref[:, lanes(t)], KERNEL * KERNEL)
+    for t in range(SUB):
+        for row, ref in ((0, gain_ref), (1, shift_ref)):
+            if t < LT:
+                v = ref[:, lanes(t)]
+                if t == LT - 1 and tail < LANES:
+                    v = jnp.concatenate([v, jnp.zeros((1, LANES - tail), F32)], axis=1)
+            else:
+                v = jnp.zeros((1, LANES), F32)
+            gc[row * SUB + t : row * SUB + t + 1, :] = v
+
+    loads[0].wait()
+    cells_from(xc, lambda t: x_nat[:, lanes(t)], CELLS)
+
+    def make_strips(src):
+        strip_top[...] = src[0 : EDGE * SUB, :].astype(BF)
+        strip_bot[...] = src[(CELLS - EDGE) * SUB : CELLS * SUB, :].astype(BF)
+        lef, rig = [], []
+        for r in range(TILE_SIDE):
+            row = r * TILE_SIDE * SUB
+            lef.append(src[row : row + MARGIN * SUB, :])
+            rig.append(src[row + (TILE_SIDE - MARGIN) * SUB : row + TILE_SIDE * SUB, :])
+        strip_lef[...] = jnp.concatenate(lef, axis=0).astype(BF)
+        strip_rig[...] = jnp.concatenate(rig, axis=0).astype(BF)
+
+    def halo_up(e, k):
+        return remote(strip_bot, from_low.at[e, k], halo_send.at[e, 0, k], halo_recv.at[e, 0, k], me + k)
+
+    def halo_down(e, k):
+        return remote(strip_top, from_high.at[e, k], halo_send.at[e, 1, k], halo_recv.at[e, 1, k], me - k)
+
+    def halo_east(e):
+        return remote(strip_rig, from_w.at[e, 1], halo_send.at[e, 0, 0], halo_recv.at[e, 0, 0], me + 1)
+
+    def halo_west(e):
+        return remote(strip_lef, from_e.at[e, 1], halo_send.at[e, 1, 0], halo_recv.at[e, 1, 0], me - 1)
+
+    def halo_start(e):
+        @pl.loop(1, REACH + 1)
+        def _(k):
+            @pl.when(me + k < N)
+            def _():
+                halo_up(e, k).start()
+
+            @pl.when(me - k >= 0)
+            def _():
+                halo_down(e, k).start()
+
+        @pl.when(me + 1 < N)
+        def _():
+            halo_east(e).start()
+
+        @pl.when(me >= 1)
+        def _():
+            halo_west(e).start()
+
+    def halo_wait(e):
+        @pl.loop(1, REACH + 1)
+        def _(k):
+            @pl.when(me + k < N)
+            def _():
+                halo_up(e, k).wait_send()
+                halo_down(e, k).wait_recv()
+
+            @pl.when(me - k >= 0)
+            def _():
+                halo_down(e, k).wait_send()
+                halo_up(e, k).wait_recv()
+
+        @pl.when(me + 1 < N)
+        def _():
+            halo_east(e).wait_send()
+            halo_west(e).wait_recv()
+
+        @pl.when(me >= 1)
+        def _():
+            halo_west(e).wait_send()
+            halo_east(e).wait_recv()
+
+    zero_strip = jnp.zeros((EDGE * SUB, LANES), BF)
+    for e in range(2):
+        from_low[e, 0] = zero_strip
+        from_high[e, 0] = zero_strip
+        from_w[e, 0] = zero_strip
+        from_e[e, 0] = zero_strip
+
+    def fill_pad(e, centre):
+        def low_slot(d):
+            n = nbr_ref[0, d]
+            return jnp.clip(jnp.where(n < 0, 0, me - lax.shift_right_arithmetic(n, 1)), 0, REACH)
+
+        def high_slot(d):
+            n = nbr_ref[0, d]
+            return jnp.clip(jnp.where(n < 0, 0, lax.shift_right_arithmetic(n, 1) - me), 0, REACH)
+
+        def there(d):
+            return jnp.where(nbr_ref[0, d] < 0, 0, 1)
+
+        def put(row, col, value):
+            at = (row * PAD_SIDE + col) * SUB
+            pad[at : at + value.shape[0], :] = value
+
+        S, M, T = SUB, MARGIN, TILE_SIDE
+        for which, refs, slot, d3, row0 in (
+            ("low", from_low, low_slot, (0, 1, 2), 0),
+            ("high", from_high, high_slot, (5, 6, 7), M + T),
+        ):
+            left = refs[e, slot(d3[0])].astype(F32)
+            mid = refs[e, slot(d3[1])].astype(F32)
+            right = refs[e, slot(d3[2])].astype(F32)
+            for r in range(M):
+                at = r * T * S
+                put(row0 + r, 0, left[at + (T - M) * S : at + T * S])
+                put(row0 + r, M, mid[at : at + T * S])
+                put(row0 + r, M + T, right[at : at + M * S])
+        west = from_w[e, there(3)].astype(F32)
+        east = from_e[e, there(4)].astype(F32)
+        for r in range(T):
+            put(M + r, 0, west[r * M * S : (r + 1) * M * S])
+            put(M + r, M, centre[r * T * S : (r + 1) * T * S, :])
+            put(M + r, M + T, east[r * M * S : (r + 1) * M * S])
+
+    make_strips(xc)
+    n_partners = jnp.minimum(REACH, N - 1 - me) + jnp.minimum(REACH, me) + (Q - 1)
+    pl.semaphore_wait(barrier, n_partners)
+    halo_start(0)
+
+    eye = lax.broadcasted_iota(jnp.int32, (CELLS, CELLS), 0) == lax.broadcasted_iota(jnp.int32, (CELLS, CELLS), 1)
+    mask_row = maskv_ref[0:1, :].astype(F32)
+    mask_col = jnp.sum(jnp.where(eye, mask_row, 0.0), axis=1, keepdims=True)
+    n_mine = jnp.sum(mask_row)
+    loads[1].wait()
+    ups[...] = (cot_nat[...] * mask_col).astype(BF)
+    loads[2].wait()
+    chunk = 5 * LANES
+
+    @pl.loop(0, H // chunk)
+    def _(i):
+        at = pl.multiple_of(i * chunk, chunk)
+        actg[:, pl.ds(at, chunk)] = dot(ups[...], wout[pl.ds(at, chunk), :], NT)
+
+    loads[3].wait()
+    for b in range(Q):
+        start = b * (H // Q) + p * hb
+        first, width = window(start, hb, H)
+        pick_row = lax.broadcasted_iota(jnp.int32, (LANES, width), 0)
+        pick_col = lax.broadcasted_iota(jnp.int32, (LANES, width), 1)
+        first = pl.multiple_of(first, LANES)
+        pick = ((pick_col == pick_row + (start - first)) & (pick_row < hb)).astype(F32)
+        pick_low = pick.astype(BF)
+        wo_t[b * LANES : (b + 1) * LANES, :] = dot(pick_low, wout[pl.ds(first, width), :]).astype(BF)
+        wi_t[b * LANES : (b + 1) * LANES, :] = dot(pick_low, win[:, pl.ds(first, width)], NT).astype(BF)
+        bi_t[b * LANES : (b + 1) * LANES, :] = jnp.sum(pick * bin_ref[:, pl.ds(first, width)], axis=1, keepdims=True)
+
+    def rows_copy(which, src, dst, s):
+        at = pl.multiple_of(p * CELLS, 16)
+        return remote(src, dst.at[pl.ds(at, CELLS)], rows_send.at[which, s], rows_recv.at[which, s], in_plane(s))
+
+    def rows_start(which, src, dst):
+        @pl.loop(1, INNER)
+        def _(s):
+            rows_copy(which, src, dst, s).start()
+
+        dst[pl.ds(pl.multiple_of(p * CELLS, 16), CELLS), :] = src[...]
+
+    def rows_wait(which, src, dst):
+        @pl.loop(1, INNER)
+        def _(s):
+            rows_copy(which, src, dst, s).wait()
+
+    rows_start(0, ups, uall)
+
+    halo_wait(0)
+    fill_pad(0, xc)
+
+    def depthwise(dst, flip):
+        @pl.loop(0, TILE_SIDE)
+        def _(r):
+            acc = [None] * TILE_SIDE
+            for a in range(KERNEL):
+                base = pl.multiple_of((r + a) * (PAD_SIDE * SUB), SUB)
+                row = [pad[pl.ds(base + j * SUB, SUB), :] for j in range(PAD_SIDE)]
+                for b in range(KERNEL):
+                    tap = a * KERNEL + b
+                    if flip:
+                        tap = KERNEL * KERNEL - 1 - tap
+                    k = kc[tap * SUB : (tap + 1) * SUB, :]
+                    for c in range(TILE_SIDE):
+                        term = k * row[c + b]
+                        acc[c] = term if acc[c] is None else acc[c] + term
+            out = pl.multiple_of(r * (TILE_SIDE * SUB), SUB)
+            for c in range(TILE_SIDE):
+                dst[pl.ds(out + c * SUB, SUB), :] = acc[c]
+
+    depthwise(conv, False)
+
+    def cell_mask(i):
+        return mask_ref[0, i].astype(F32)
+
+    def over_cells(fun, init):
+        def body(r, carry):
+            at = r * TILE_SIDE
+            for c in range(TILE_SIDE):
+                rows = pl.ds(pl.multiple_of(at * SUB, SUB) + c * SUB, SUB)
+                carry = fun(at + c, rows, carry)
+            return carry
+
+        return lax.fori_loop(0, TILE_SIDE, body, init)
+
+    zero = jnp.zeros((SUB, LANES), F32)
+    my_sum = over_cells(lambda i, rows, acc: acc + conv[rows, :] * cell_mask(i), zero)
+    my_mean = my_sum / n_mine
+
+    def deviation(i, rows, acc):
+        d = conv[rows, :] - my_mean
+        return acc + d * d * cell_mask(i)
+
+    my_dev = over_cells(deviation, zero)
+    sub_row = lax.broadcasted_iota(jnp.int32, (SUB, LANES), 0)
+
+    def put_moments(ref, total, dev, count):
+        ref[0:SUB, :] = jnp.where(sub_row == SUB - 1, count, total)
+        ref[SUB : 2 * SUB, :] = dev
+
+    def vec_exchange(e, src, slots):
+        def copy(s):
+            return remote(src, slots.at[s], vec_send.at[e, s], vec_recv.at[e, s], in_plane(s))
+
+        @pl.loop(1, INNER)
+        def _(s):
+            copy(s).start()
+
+        @pl.loop(1, INNER)
+        def _(s):
+            copy(s).wait()
+
+    def col_exchange(e, src, slots):
+        def copy(t):
+            return remote(src, slots.at[t], col_send.at[e, t], col_recv.at[e, t], in_column(t))
+
+        @pl.loop(1, Q)
+        def _(t):
+            copy(t).start()
+
+        @pl.loop(1, Q)
+        def _(t):
+            copy(t).wait()
+
+    def merge_moments(src, slots, count):
+        msgs = [src[...]] + [slots[s] for s in range(1, count)]
+        counts = [m[SUB - 1 : SUB, :] for m in msgs]
+        total, n = msgs[0][0:SUB], counts[0]
+        for m, c in zip(msgs[1:], counts[1:]):
+            total, n = total + m[0:SUB], n + c
+        mean = total / n
+        dev = zero
+        for m, c in zip(msgs, counts):
+            off = m[0:SUB] / c - mean
+            dev = dev + m[SUB : 2 * SUB] + c * off * off
+        return total, dev, n, mean
+
+    put_moments(stat_sa.at[0], my_sum, my_dev, n_mine)
+    vec_exchange(0, stat_sa.at[0], stat_a.at[0])
+    plane_sum, plane_dev, plane_n, _ = merge_moments(stat_sa.at[0], stat_a.at[0], INNER)
+    put_moments(stat_sb.at[0], plane_sum, plane_dev, plane_n)
+    col_exchange(0, stat_sb.at[0], stat_b.at[0])
+    _, all_dev, n_row, mean = merge_moments(stat_sb.at[0], stat_b.at[0], Q)
+    inv = lax.rsqrt(all_dev / n_row + EPSILON)
+    gain_c = gc[0:SUB, :]
+    scale_c = inv * gain_c
+    inv_n = 1.0 / n_row
+
+    for t in range(LT):
+        v = conv[pl.ds(t, CELLS, stride=SUB), :]
+        v = (v - mean[t : t + 1]) * inv[t : t + 1] * gain_c[t : t + 1] + gc[SUB + t : SUB + t + 1, :]
+        if t == LT - 1:
+            v = v[:, :tail]
+        nrm[:, lanes(t)] = v.astype(BF)
+    rows_start(1, nrm, nall)
+
+    kg[...] = jnp.zeros_like(kg)
+    taps = KERNEL * KERNEL * SUB
+    branch[...] = jnp.zeros_like(branch)
+    x_rows = CELLS
+    ng = cot_nat
+
+    @pl.loop(0, H // chunk)
+    def _(i):
+        at = pl.multiple_of(i * chunk, chunk)
+        cols = pl.ds(at, chunk)
+        pre = dot(nrm[...], win[:, cols]) + bin_ref[:, cols]
+        half = 0.5 * (1.0 + lax.erf(pre * SQRT_HALF))
+        act = (pre * half).astype(BF)
+        slope = half + pre * INV_ROOT_TAU * jnp.exp(-0.5 * pre * pre)
+        pg = (actg[:, cols] * slope).astype(BF)
+        branch[...] += dot(act, wout[cols, :])
+        part = dot(pg, win[:, cols], NT)
+
+        @pl.when(i == 0)
+        def _():
+            ng[...] = part
+
+        @pl.when(i > 0)
+        def _():
+            ng[...] += part
+
+        bias = jnp.sum(pg.astype(F32), axis=0, keepdims=True)
+        for j in range(chunk // LANES):
+            kg[pl.ds(taps + i * (chunk // LANES) + j, 1), :] = bias[:, j * LANES : (j + 1) * LANES]
+
+    o_block[...] = (x_nat[...] + branch[...] + bout_ref[...]) * mask_col
+    ob = jnp.sum(ups[...].astype(F32), axis=0, keepdims=True)
+    bias_rows = -(-(H // LANES) // SUB) * SUB
+    for t in range(LT):
+        v = ob[:, lanes(t)]
+        if t == LT - 1 and tail < LANES:
+            v = jnp.concatenate([v, jnp.zeros((1, LANES - tail), F32)], axis=1)
+        kg[taps + bias_rows + t : taps + bias_rows + t + 1, :] = v
+
+    cells_from(ngc, lambda t: ng[:, lanes(t)], CELLS)
+
+    def grads(i, rows, carry):
+        g = ngc[rows, :]
+        return carry[0] + g, carry[1] + g * ((conv[rows, :] - mean) * inv)
+
+    shift_part, gain_part = over_cells(grads, (zero, zero))
+    stat_sa[1, 0:SUB, :] = shift_part
+    stat_sa[1, SUB : 2 * SUB, :] = gain_part
+    vec_exchange(1, stat_sa.at[1], stat_a.at[1])
+    tot = stat_sa[1]
+    for s in range(1, INNER):
+        tot = tot + stat_a[1, s]
+    stat_sb[1] = tot
+    col_exchange(1, stat_sb.at[1], stat_b.at[1])
+    for t in range(1, Q):
+        tot = tot + stat_b[1, t]
+    shift_grad, gain_grad = tot[0:SUB], tot[SUB : 2 * SUB]
+    o_vec[0 : 2 * SUB, :] = tot
+
+    def to_conv_grad(r, _):
+        at = r * TILE_SIDE
+        for c in range(TILE_SIDE):
+            rows = pl.ds(pl.multiple_of(at * SUB, SUB) + c * SUB, SUB)
+            scaled = (conv[rows, :] - mean) * inv
+            ngc[rows, :] = scale_c * (
+                ngc[rows, :] - cell_mask(at + c) * (shift_grad + scaled * gain_grad) * inv_n
+            )
+        return 0
+
+    lax.fori_loop(0, TILE_SIDE, to_conv_grad, 0)
+    make_strips(ngc)
+    halo_start(1)
+
+    @pl.loop(0, KERNEL)
+    def _(a):
+        acc = [zero] * KERNEL
+        for r in range(TILE_SIDE):
+            base = pl.multiple_of((r + a) * (PAD_SIDE * SUB), SUB)
+            row = [pad[pl.ds(base + j * SUB, SUB), :] for j in range(PAD_SIDE)]
+            for c in range(TILE_SIDE):
+                g = ngc[(r * TILE_SIDE + c) * SUB : (r * TILE_SIDE + c + 1) * SUB, :]
+                for b in range(KERNEL):
+                    acc[b] = acc[b] + g * row[c + b]
+        for b in range(KERNEL):
+            at = pl.multiple_of(a * (KERNEL * SUB), SUB)
+            kg[pl.ds(at + b * SUB, SUB), :] = acc[b]
+
+    rows_wait(0, ups, uall)
+    rows_wait(1, nrm, nall)
+    part_rows = 3 * LANES
+
+    @pl.loop(0, INNER * CELLS // part_rows)
+    def _(i):
+        at = pl.multiple_of(i * part_rows, part_rows)
+        rows = pl.ds(at, part_rows)
+        pre = dot(wi_t[...], nall[rows, :], NT) + bi_t[...]
+        half = 0.5 * (1.0 + lax.erf(pre * SQRT_HALF))
+        act_t[:, rows] = (pre * half).astype(BF)
+        slope = half + pre * INV_ROOT_TAU * jnp.exp(-0.5 * pre * pre)
+        pg_t[:, rows] = (dot(wo_t[...], uall[rows, :], NT) * slope).astype(BF)
+
+    og[...] = dot(act_t[...], uall[...])
+    zrows = zo_src.shape[1]
+    for b in range(Q):
+        zo_src[b] = og[b * LANES : b * LANES + zrows, :].astype(BF)
+
+    def zo_copy(t):
+        return remote(zo_src.at[lax.rem(q + t, Q)], zo_dst.at[t], z_send.at[0, t], z_recv.at[0, t], in_column(t))
+
+    def zi_copy(t):
+        return remote(zi_src.at[lax.rem(q + t, Q)], zi_dst.at[t], z_send.at[1, t], z_recv.at[1, t], in_column(t))
+
+    @pl.loop(1, Q)
+    def _(t):
+        zo_copy(t).start()
+
+    ig[...] = dot(pg_t[...], nall[...])
+    cq = C // Q
+    for b in range(Q):
+        zi_src[b] = ig[:, b * cq : (b + 1) * cq].astype(BF)
+
+    @pl.loop(1, Q)
+    def _(t):
+        zi_copy(t).start()
+
+    halo_wait(1)
+    fill_pad(1, ngc)
+    depthwise(conv, True)
+    for t in range(LT):
+        v = conv[pl.ds(t, CELLS, stride=SUB), :]
+        if t == LT - 1:
+            v = v[:, :tail]
+        o_fgrad[:, lanes(t)] = v
+
+    part = kg.shape[0] // INNER
+
+    def ks_copy(s):
+        to = lax.rem(p + s, INNER)
+        return remote(
+            kg.at[pl.ds(pl.multiple_of(to * part, SUB), part)], kg_slot.at[s], ks_send.at[0, s], ks_recv.at[0, s], in_plane(s)
+        )
+
+    def kc_copy(t):
+        return remote(kg_col.at[0], kg_col.at[t], ks_send.at[1, t], ks_recv.at[1, t], in_column(t))
+
+    def kt_copy(s):
+        at = pl.ds(pl.multiple_of(p * part, SUB), part)
+        return remote(kg_tot.at[at], kg_tot.at[at], ks_send.at[2, s], ks_recv.at[2, s], in_plane(s))
+
+    def run(lo, hi, copy):
+        @pl.loop(lo, hi)
+        def _(s):
+            copy(s).start()
+
+        @pl.loop(lo, hi)
+        def _(s):
+            copy(s).wait()
+
+    run(1, INNER, ks_copy)
+    mine = pl.ds(pl.multiple_of(p * part, SUB), part)
+    tot = kg[mine, :]
+    for s in range(1, INNER):
+        tot = tot + kg_slot[s]
+    kg_col[0] = tot
+    run(1, Q, kc_copy)
+    for t in range(1, Q):
+        tot = tot + kg_col[t]
+    kg_tot[mine, :] = tot
+    run(1, INNER, kt_copy)
+    for t in range(LT):
+        o_kgrad[:, lanes(t)] = kg_tot[pl.ds(t, KERNEL * KERNEL, stride=SUB), :][:, : (tail if t == LT - 1 else LANES)]
+    o_vec[2 * SUB : 2 * SUB + bias_rows + SUB, :] = kg_tot[taps : taps + bias_rows + SUB, :]
+
+    @pl.loop(1, Q)
+    def _(t):
+        zo_copy(t).wait()
+        zi_copy(t).wait()
+
+    own = og[pl.ds(pl.multiple_of(q * LANES, LANES), zrows), :]
+    for t in range(1, Q):
+        own = own + zo_dst[t].astype(F32)
+    o_wout[...] = own[:hb]
+
+    tr[...] = zi_src[q].astype(F32)
+    for t in range(1, Q):
+        tr[...] += zi_dst[t].astype(F32)
+    flat = tr[...]
+    flat = jnp.concatenate([flat, jnp.zeros((flat.shape[0], 2 * LANES - cq), F32)], axis=1)
+    flat = flat.T
+    for d in range(INNER):
+        tr_src[d] = flat[d * cb : d * cb + tr_src.shape[1], :]
+
+    def tr_copy(s):
+        to = lax.rem(p + s, INNER)
+        return remote(tr_src.at[to], tr_dst.at[p], tr_send.at[s], tr_recv.at[s], in_plane(s))
+
+    @pl.loop(1, INNER)
+    def _(s):
+        tr_copy(s).start()
+
+    tr_dst[p] = tr_src[p]
+
+    @pl.loop(1, INNER)
+    def _(s):
+        tr_copy(s).wait()
+
+    pieces = []
+    for b in range(Q):
+        for d in range(INNER):
+            pieces.append(tr_dst[d, :, b * LANES : b * LANES + hb])
+    o_win[...] = jnp.concatenate(pieces, axis=1)[:cb]
+
+
+def run_step(N, fields, cotangent, kernel, norm_gain, norm_shift, weight_in, bias_in, weight_out, bias_out, neighbours, land_mask):
+    C = fields.shape[-1]
+    H = weight_in.shape[1]
+    Q = N // INNER
+    hb, cb = H // N, C // N
+    LT = -(-C // LANES)
+    any_ = pl.BlockSpec(memory_space=pl.ANY)
+    vmem = pl.BlockSpec(memory_space=pltpu.VMEM)
+    smem = pl.BlockSpec(memory_space=pltpu.SMEM)
+    bias_rows = -(-(H // LANES) // SUB) * SUB
+    kg_rows = KERNEL * KERNEL * SUB + bias_rows + SUB
+    kg_rows = -(-kg_rows // (INNER * SUB)) * INNER * SUB
+    zrows = -(-hb // 16) * 16
+    V, D = pltpu.VMEM, pltpu.SemaphoreType.DMA
+    tr_rows = -(-cb // SUB) * SUB
+    outs = (
+        jax.ShapeDtypeStruct((CELLS, C), F32),
+        jax.ShapeDtypeStruct((CELLS, C), F32),
+        jax.ShapeDtypeStruct((KERNEL * KERNEL, C), F32),
+        jax.ShapeDtypeStruct((3 * SUB + bias_rows, LANES), F32),
+        jax.ShapeDtypeStruct((cb, H), F32),
+        jax.ShapeDtypeStruct((hb, C), F32),
+    )
+    cell = (CELLS * SUB, LANES)
+    strip = (EDGE * SUB, LANES)
+    scratch = [
+        V((CELLS, C), F32),
+        V((CELLS, C), F32),
+        V((C, H), BF),
+        V((H, C), BF),
+        V(cell, F32),
+        V((PAD_SIDE * PAD_SIDE * SUB, LANES), F32),
+        V(cell, F32),
+        V(cell, F32),
+        V((KERNEL * KERNEL * SUB, LANES), F32),
+        V((2 * SUB, LANES), F32),
+        V(strip, BF),
+        V(strip, BF),
+        V(strip, BF),
+        V(strip, BF),
+        V((2, REACH + 1) + strip, BF),
+        V((2, REACH + 1) + strip, BF),
+        V((2, 2) + strip, BF),
+        V((2, 2) + strip, BF),
+        V((2, INNER, 2 * SUB, LANES), F32),
+        V((2, Q, 2 * SUB, LANES), F32),
+        V((2, 2 * SUB, LANES), F32),
+        V((2, 2 * SUB, LANES), F32),
+        V((CELLS, C), BF),
+        V((CELLS, C), BF),
+        V((CELLS, H), F32),
+        V((CELLS, C), F32),
+        V((INNER * CELLS, C), BF),
+        V((INNER * CELLS, C), BF),
+        V((Q * LANES, C), BF),
+        V((Q * LANES, C), BF),
+        V((Q * LANES, 1), F32),
+        V((Q * LANES, INNER * CELLS), BF),
+        V((Q * LANES, INNER * CELLS), BF),
+        V((Q * LANES, C), F32),
+        V((Q * LANES, C), F32),
+        V((Q, zrows, C), BF),
+        V((Q, Q * LANES, C // Q), BF),
+        V((Q, zrows, C), BF),
+        V((Q, Q * LANES, C // Q), BF),
+        V((Q * LANES, C // Q), F32),
+        V((INNER, tr_rows, Q * LANES), F32),
+        V((INNER, tr_rows, Q * LANES), F32),
+        V((kg_rows, LANES), F32),
+        V((INNER, kg_rows // INNER, LANES), F32),
+        V((Q, kg_rows // INNER, LANES), F32),
+        V((kg_rows, LANES), F32),
+        D((4,)),
+        D((2, 2, REACH + 1)),
+        D((2, 2, REACH + 1)),
+        D((2, INNER)),
+        D((2, INNER)),
+        D((2, Q)),
+        D((2, Q)),
+        D((2, INNER)),
+        D((2, INNER)),
+        D((2, Q)),
+        D((2, Q)),
+        D((INNER,)),
+        D((INNER,)),
+        D((3, max(INNER, Q))),
+        D((3, max(INNER, Q))),
+    ]
+    rows = CELLS
+    return pl.pallas_call(
+        functools.partial(step_kernel, N, C, H),
+        out_shape=outs,
+        in_specs=[any_, any_, vmem, vmem, vmem, any_, vmem, any_, vmem, smem, smem, vmem],
+        out_specs=[vmem] * len(outs),
+        scratch_shapes=scratch,
+        compiler_params=pltpu.CompilerParams(
+            collective_id=0, has_side_effects=True, vmem_limit_bytes=58 * 1024 * 1024
+        ),
+        cost_estimate=pl.CostEstimate(
+            flops=20 * rows * C * H, bytes_accessed=4 * C * H + 8 * rows * C, transcendentals=4 * rows * H
+        ),
+        name="step",
+    )(
+        fields,
+        cotangent,
+        kernel,
+        norm_gain.reshape(1, C),
+        norm_shift.reshape(1, C),
+        weight_in,
+        bias_in.reshape(1, H),
+        weight_out,
+        bias_out.reshape(1, C),
+        neighbours,
+        land_mask,
+        land_mask,
+    )
+
+
+def local_step(N, grad_shape, fields, cotangent, kernel, norm_gain, norm_shift, weight_in, bias_in, weight_out, bias_out, neighbours, land_mask):
+    C = fields.shape[-1]
+    H = weight_in.shape[1]
+    block, fgrad, kgrad, vec, gwin, gwout = run_step(
+        N, fields, cotangent, kernel, norm_gain, norm_shift, weight_in, bias_in, weight_out, bias_out, neighbours, land_mask
+    )
+    bias_rows = -(-(H // LANES) // SUB) * SUB
+    rest = jnp.zeros((fields.shape[0] - 1,) + block.shape, F32)
+    return (
+        jnp.concatenate([block[None], rest], axis=0),
+        jnp.concatenate([(fgrad + cotangent[0] * land_mask[0].astype(F32)[:, None])[None], rest], axis=0),
+        kgrad,
+        vec[SUB : 2 * SUB].reshape(-1)[:C],
+        vec[0:SUB].reshape(-1)[:C],
+        gwin.reshape(grad_shape),
+        vec[2 * SUB : 2 * SUB + bias_rows].reshape(-1)[:H],
+        gwout.reshape(grad_shape),
+        vec[2 * SUB + bias_rows : 3 * SUB + bias_rows].reshape(-1)[:C],
+    )
 
 
 def from_behind(shard, axis, by):
@@ -92,7 +890,7 @@
     )
 
 
-def local(
+def general(
     fields,
     cotangent,
     kernel,
@@ -181,33 +979,44 @@
     )
 
 
+IN_SPECS = (
+    P("tile", None, None),
+    P("tile", None, None),
+    P(),
+    P(),
+    P(),
+    P(),
+    P(),
+    P(),
+    P(),
+    P("tile", None),
+    P("tile", None),
+)
+OUT_SPECS = (
+    P("tile", None, None),
+    P("tile", None, None),
+    P(),
+    P(),
+    P(),
+    P("tile", None),
+    P(),
+    P("tile", None),
+    P(),
+)
+
+
 def solution(mesh):
-    return jax.shard_map(
-        local,
-        mesh=mesh,
-        in_specs=(
-            P("tile", None, None),
-            P("tile", None, None),
-            P(),
-            P(),
-            P(),
-            P(),
-            P(),
-            P(),
-            P(),
-            P("tile", None),
-            P("tile", None),
-        ),
-        out_specs=(
-            P("tile", None, None),
-            P("tile", None, None),
-            P(),
-            P(),
-            P(),
-            P("tile", None),
-            P(),
-            P("tile", None),
-            P(),
-        ),
-        check_vma=False,
-    )
+    N = mesh.shape["tile"]
+
+    def whole(fields, cotangent, kernel, norm_gain, norm_shift, weight_in, *rest):
+        C, H = weight_in.shape
+        fits = N % INNER == 0 and C % N == 0 and H % N == 0
+        if fits:
+            body = functools.partial(local_step, N, (SUB, C * H // (SUB * N)))
+        else:
+            body = general
+        return jax.shard_map(body, mesh=mesh, in_specs=IN_SPECS, out_specs=OUT_SPECS, check_vma=False)(
+            fields, cotangent, kernel, norm_gain, norm_shift, weight_in, *rest
+        )
+
+    return whole

time: 1190 us -> 170 us (0.14)
  waiting for transfers between devices: 342 us -> 0 us
  other arithmetic: 202 us -> 1.15 us
  starting transfers between devices: 195 us -> 0 us
  blocking collectives: 180 us -> 0 us
  local copies, waits for them, and re-layouts: 194 us -> 20.5 us
  Pallas kernels: 0 us -> 147 us
  matrix products: 47.6 us -> 0 us
  between operations: 16.5 us -> 0.72 us
    psum x1 -> x0, waiting for transfers between devices: 227 us -> none  [local(): kernel_grad = lax.psum(kernel_part, 'tile')]
    ppermute x28 -> x0, starting transfers between devices: 195 us -> none  [from_behind(): return lax.ppermute(shard, axis, pairs)]
    psum x3 -> x0, blocking collectives: 180 us -> none  [the longest x1 98 us: local(): lax.psum((jnp.sum(ocean), jnp.sum(conv * cell_weight, axis=(0, 1))), 'tile')]
    pallas_call x0 -> x1, Pallas kernels: none -> 147 us  [run_step(): pl.pallas_call(functools.partial(step_kernel, N, C, H), out_shape=outs, i...]
    ppermute x28 -> x0, waiting for transfers between devices: 115 us -> none  [from_behind(): return lax.ppermute(shard, axis, pairs)]
    add_any x3 -> x0, other arithmetic: 82.6 us -> none  [the longest x1 75.2 us: depthwise(): padded[:, row_tap:row_tap + tile_side, col_tap:col_tap + tile_side]]
    reduce_sum x8 -> x0, other arithmetic: 80.3 us -> none  [the longest x4 40.5 us: depthwise(): kernel[row_tap * KERNEL + col_tap]]
    dot_general x7 -> x0, matrix products: 47.6 us -> none  [the longest x1 14.8 us: local(): jnp.dot(choose, nearby_grad.reshape(slots * 8, -1), precision=lax.Precisi...]
  transfers between devices with their start and end apart: 29 -> 0, of which waited for: 9 -> 0; matrix products, arithmetic and copies ran while one was open for 8% -> 0% of each run, Pallas kernels for 0% -> 0%
where the time goes in v1:
time: 170 us; the launch traced here: 169 us
  Pallas kernels  147 us (86%)
  local copies, waits for them, and re-layouts  20.5 us (12%)
    pallas_call x1, Pallas kernels, run_step(): pl.pallas_call(functools.partial(step_kernel, N, C, H), out_shape=outs, i...  147 us
    unnamed x18, local copies, waits for them, and re-layouts  9.36 us

profile of v1, /device:TPU:0, one launch (start us, length us, event | category | flops | bytes accessed | tf_op | source)
XLA Modules:
  0.0 169.2 jit_solution(9853730546226609183)
XLA Ops:
  0.6 0.0 copy-start.3
  0.7 0.0 copy-start.4
  0.7 0.0 copy-start.5
  0.7 0.0 copy-start.6
  0.7 8.6 %copy.20.wout_hbm = bf16[3200,800]{1,0:T(8,128)(2,1)} copy(bf16[3200,800]{0,1:T(8,128)(2,1)} %param.18) | data formatting | bytes 10240000 | tf_op args[7]
  9.3 0.0 copy-done.3
  9.3 0.6 reshape.55.bin_ref
  9.9 0.0 copy-done.4
  9.9 0.6 reshape.53.gain_ref
  10.5 0.0 copy-done.5
  10.5 0.6 reshape.54.shift_ref
  11.1 0.0 copy-done.6
  11.1 0.6 reshape.56.bout_ref
  11.7 0.0 copy-start.7
  11.7 0.0 copy-start.1
  11.7 146.8 %step.1 = (f32[144,800]{1,0:T(8,128)}, f32[144,800]{1,0:T(8,128)}, f32[49,800]{1,0:T(8,128)}, f32[56,128]{1,0:T(8,128)}, f32[25,3200]{1,0:T(8,128)}, /*index=5*/f32[100,800]{1,0:T(8,128)}) custom-call(f32[2,144,800]{2,1,0:T(8,128)} %fields_hbm.1, f32[2,144,800]{2,1,0:T(8,128)} %cot_hbm.1, f32[49,800]{1,0:T(8,128)} %kernel_ref.1, f32[1,800]{1,0:T(1,128)} %reshape.53.gain_ref, ...), custom_call_target="tpu_custom_call" | custom-call | flops 7372800000 | bytes 11161600 | tf_op jit(solution)/shard_map/step/pallas_call | solution.py:765
  158.5 0.0 copy-start
  158.5 0.0 copy-start.2
  158.5 1.4 slice_bitcast_fusion.1
  159.9 1.3 slice_bitcast_fusion
  161.2 0.0 copy-done.7
  161.2 0.0 copy-done.1
  161.2 1.1 fusion.1
  162.4 1.0 concatenate.7
  163.4 2.1 %concatenate.6 = f32[2,144,800]{2,1,0:T(8,128)} pad(f32[1,144,800]{2,1,0:T(8,128)} %bitcast.21, f32[]{:T(128)} %constant.0.clone.1), padding=0_1x0_0x0_0 | pad | bytes 1382404 | tf_op jit(solution)/shard_map/concatenate | solution.py:803
  165.5 2.0 %reshape.59 = f32[8,10000]{1,0:T(8,128)} reshape(f32[25,3200]{1,0:T(8,128)} %get-tuple-element.19) | data formatting | bytes 640000 | tf_op jit(solution)/shard_map/reshape | solution.py:808
  167.5 0.0 copy-done
  167.5 1.0 reshape.60
  168.5 0.0 copy-done.2
  168.5 0.7 copy.22
  (1 shorter events, 0.0 us)
Async XLA Ops:
  0.6 8.7 %copy-start.3 = (f32[3200]{0:T(1024)S(1)}, f32[3200]{0:T(1024)}, u32[]{:S(2)}) copy-start(f32[3200]{0:T(1024)} %param.17) | copy-start | bytes 38404
  0.7 9.3 %copy-start.4 = (f32[800]{0:T(1024)S(1)}, f32[800]{0:T(1024)}, u32[]{:S(2)}) copy-start(f32[800]{0:T(1024)} %param.14) | copy-start | bytes 9604
  0.7 9.9 %copy-start.5 = (f32[800]{0:T(1024)S(1)}, f32[800]{0:T(1024)}, u32[]{:S(2)}) copy-start(f32[800]{0:T(1024)} %param.15) | copy-start | bytes 9604
  0.7 10.4 %copy-start.6 = (f32[800]{0:T(1024)S(1)}, f32[800]{0:T(1024)}, u32[]{:S(2)}) copy-start(f32[800]{0:T(1024)} %param.19) | copy-start | bytes 9604
  11.7 149.5 %copy-start.7 = (s32[2,144]{1,0:T(2,128)S(1)}, s32[2,144]{1,0:T(2,128)}, u32[]{:S(2)}) copy-start(s32[2,144]{1,0:T(2,128)} %maskv_ref.1) | copy-start | bytes 3460
  11.7 149.5 %copy-start.1 = (f32[2,144,800]{2,1,0:T(8,128)S(1)}, f32[2,144,800]{2,1,0:T(8,128)}, u32[]{:S(2)}) copy-start(f32[2,144,800]{2,1,0:T(8,128)} %cot_hbm.1) | copy-start | bytes 2764804
  158.5 9.0 %copy-start = (f32[100,800]{1,0:T(8,128)S(1)}, f32[100,800]{1,0:T(8,128)}, u32[]{:S(2)}) copy-start(f32[100,800]{1,0:T(8,128)} %get-tuple-element.20) | copy-start | bytes 960004
  158.5 10.0 %copy-start.2 = (f32[49,800]{1,0:T(8,128)S(1)}, f32[49,800]{1,0:T(8,128)}, u32[]{:S(2)}) copy-start(f32[49,800]{1,0:T(8,128)} %get-tuple-element.35) | copy-start | bytes 470404

commit v2 on v0

--- a/solution.py
+++ b/solution.py
@@ -1,17 +1,1031 @@
+import functools
+import types
+
 import jax
 import jax.numpy as jnp
 from jax import lax
+from jax.experimental import pallas as pl
+from jax.experimental.pallas import tpu as pltpu
 from jax.sharding import PartitionSpec as P
 
 TILE_SIDE = 12
 KERNEL = 7
 CELLS = 144
 REACH = 7
-
+MARGIN = KERNEL // 2
+PAD_SIDE = TILE_SIDE + 2 * MARGIN
+EDGE = MARGIN * TILE_SIDE
+TAPS = KERNEL * KERNEL
+INNER = 8
+CHIPS = INNER // 2
+LANES = 128
+SUB = 8
 
 EPSILON = 1e-05
 SQRT_HALF = 0.7071067811865476
 INV_ROOT_TAU = 0.3989422804014327
+BF = jnp.bfloat16
+F32 = jnp.float32
+MESH = pl.DeviceIdType.MESH
+NN = (((1,), (0,)), ((), ()))
+NT = (((1,), (1,)), ((), ()))
+
+
+def dot(a, b, dims=NN):
+    return lax.dot_general(a, b, dims, preferred_element_type=F32)
+
+
+def gelu_parts(pre):
+    half = 0.5 * (1.0 + lax.erf(pre * SQRT_HALF))
+    return pre * half, half + pre * INV_ROOT_TAU * jnp.exp(-0.5 * pre * pre)
+
+
+def pad_lanes(v, width):
+    if v.shape[1] == width:
+        return v
+    return jnp.concatenate([v, jnp.zeros((v.shape[0], width - v.shape[1]), v.dtype)], axis=1)
+
+
+class Sizes:
+    def __init__(self, N, C, H):
+        self.N, self.C, self.H = N, C, H
+        self.Q = N // INNER
+        self.chips = N // 2
+        self.hb, self.cb = H // N, C // N
+        self.hq, self.cq = self.hb * self.Q, C // self.Q
+        self.LT = -(-C // LANES)
+        self.blocks = self.Q + 1
+        self.pack_rows = self.hq // self.blocks
+        self.pack_lanes = -(-self.blocks * self.cq // LANES) * LANES
+        self.bias_rows = -(-(H // LANES) // SUB) * SUB
+        rows = TAPS * SUB + self.bias_rows + SUB
+        self.kg_rows = -(-rows // (INNER * SUB)) * INNER * SUB
+        self.tr_lanes = -(-self.hq // LANES) * LANES
+        self.half_rows = CHIPS * CELLS
+        self.out_rows = -(-self.hb // SUB) * SUB
+        self.in_rows = -(-self.cb // SUB) * SUB
+
+    @staticmethod
+    def fits(N, C, H):
+        if N % INNER or C % N or H % N or H % (5 * LANES) or C > SUB * LANES or N <= INNER:
+            return False
+        s = Sizes(N, C, H)
+        return s.hq % (16 * s.blocks) == 0 and s.cq <= 2 * LANES and s.hq <= s.Q * LANES
+
+
+def scratch_of(s):
+    V, D = pltpu.VMEM, pltpu.SemaphoreType.DMA
+    C, H, Q = s.C, s.H, s.Q
+    cell = (CELLS * SUB, LANES)
+    strip = (EDGE * SUB, LANES)
+    pack = (s.pack_rows, s.pack_lanes)
+    return dict(
+        x_nat=V((CELLS, C), F32),
+        cot_nat=V((CELLS, C), F32),
+        win=V((C, H), BF),
+        wout=V((C, H), BF),
+        xc=V(cell, F32),
+        pad=V((PAD_SIDE * PAD_SIDE * SUB, LANES), F32),
+        conv=V(cell, F32),
+        ngc=V(cell, F32),
+        kc=V((TAPS * SUB, LANES), F32),
+        gc=V((2 * SUB, LANES), F32),
+        strip_top=V(strip, BF),
+        strip_bot=V(strip, BF),
+        strip_lef=V(strip, BF),
+        strip_rig=V(strip, BF),
+        from_low=V((2, REACH + 1) + strip, BF),
+        from_high=V((2, REACH + 1) + strip, BF),
+        from_w=V((2, 2) + strip, BF),
+        from_e=V((2, 2) + strip, BF),
+        stat_a=V((2, INNER, 2 * SUB, LANES), F32),
+        stat_b=V((2, Q, 2 * SUB, LANES), F32),
+        stat_sa=V((2, 2 * SUB, LANES), F32),
+        stat_sb=V((2, 2 * SUB, LANES), F32),
+        nrm=V((CELLS, C), BF),
+        dev=V((CELLS, C), BF),
+        ups=V((CELLS, C), BF),
+        actg=V((CELLS, H), F32),
+        branch=V((CELLS, C), F32),
+        ng=V((CELLS, C), F32),
+        nall=V((2, s.half_rows, C), BF),
+        uall=V((2, s.half_rows, C), BF),
+        wi_t=V((s.hq, C), BF),
+        wo_t=V((s.hq, C), BF),
+        bi_t=V((Q * LANES, 1), F32),
+        act_t=V((2, s.hq, s.half_rows), BF),
+        pg_t=V((2, s.hq, s.half_rows), BF),
+        big=V((Q * LANES, C), F32),
+        zsrc=V((2, Q) + pack, BF),
+        zown=V((2,) + pack, F32),
+        zup=V((2, Q) + pack, BF),
+        zdn=V((2, Q) + pack, BF),
+        tr=V((2 * LANES, s.tr_lanes), F32),
+        tr_src=V((INNER, s.in_rows, s.tr_lanes), F32),
+        tr_dst=V((INNER, s.in_rows, s.tr_lanes), F32),
+        kg=V((s.kg_rows, LANES), F32),
+        kg_slot=V((INNER, s.kg_rows // INNER, LANES), F32),
+        kg_col=V((Q, s.kg_rows // INNER, LANES), F32),
+        kg_tot=V((INNER, s.kg_rows // INNER, LANES), F32),
+        tiles=V((max(s.LT * s.out_rows, -(-H // LANES) * s.in_rows), LANES), F32),
+        long=V((-(-C * H // (SUB * s.N) // LANES) * SUB, LANES), F32),
+        load_sem=D((4,)),
+        halo_send=D((2, 2, 9)),
+        halo_recv=D((2, 2, REACH + 1)),
+        side_send=D((2, 2)),
+        side_recv=D((2, 2)),
+        vec_send=D((2,)),
+        vec_recv=D((2,)),
+        col_send=D((2,)),
+        col_recv=D((2,)),
+        rows_send=D((2, 9)),
+        rows_recv=D((2, 9)),
+        z_send=D((2, Q)),
+        z_up=D((2, Q)),
+        z_dn=D((2, Q)),
+        tr_send=D((1,)),
+        tr_recv=D((1,)),
+        ks_send=D((3,)),
+        ks_recv=D((3,)),
+        out_sem=D((2,)),
+    )
+
+
+def step_kernel(s, names, *refs):
+    (
+        fields_hbm,
+        cot_hbm,
+        kernel_ref,
+        gain_ref,
+        shift_ref,
+        win_hbm,
+        bin_ref,
+        wout_hbm,
+        bout_ref,
+        nbr_ref,
+        mask_ref,
+        maskv_ref,
+        o_block,
+        o_fgrad,
+        o_kgrad,
+        o_gain,
+        o_shift,
+        o_win,
+        o_bin,
+        o_wout,
+        o_bout,
+    ) = refs[:21]
+    m = types.SimpleNamespace(**dict(zip(names, refs[21:], strict=True)))
+    N, C, H, Q, hb, cb, LT = s.N, s.C, s.H, s.Q, s.hb, s.cb, s.LT
+    hq, cq = s.hq, s.cq
+    tail = C - (LT - 1) * LANES
+    me = lax.axis_index("tile")
+    p = lax.rem(me, INNER)
+    q = me // INNER
+    chip = me // 2
+    core = lax.rem(me, 2)
+    j = lax.rem(chip, CHIPS)
+    twin = me + 1 - 2 * core
+
+    def remote(src, dst, ssem, rsem, dev):
+        return pltpu.make_async_remote_copy(
+            src_ref=src, dst_ref=dst, send_sem=ssem, recv_sem=rsem, device_id=(dev,), device_id_type=MESH
+        )
+
+    def in_plane(k):
+        return q * INNER + lax.rem(p + k, INNER)
+
+    def in_column(t):
+        return lax.rem(q + t, Q) * INNER + p
+
+    def lanes(t):
+        return slice(t * LANES, min((t + 1) * LANES, C))
+
+    loads = [
+        pltpu.make_async_copy(fields_hbm.at[0], m.x_nat, m.load_sem.at[0]),
+        pltpu.make_async_copy(cot_hbm.at[0], m.cot_nat, m.load_sem.at[1]),
+        pltpu.make_async_copy(wout_hbm, m.wout, m.load_sem.at[2]),
+        pltpu.make_async_copy(win_hbm, m.win, m.load_sem.at[3]),
+    ]
+    loads[0].start()
+    barrier = pltpu.get_barrier_semaphore()
+
+    @pl.loop(1, REACH + 1)
+    def _(k):
+        @pl.when(me + k < N)
+        def _():
+            pl.semaphore_signal(barrier, inc=1, device_id=(me + k,), device_id_type=MESH)
+
+        @pl.when(me - k >= 0)
+        def _():
+            pl.semaphore_signal(barrier, inc=1, device_id=(me - k,), device_id_type=MESH)
+
+    @pl.loop(1, Q)
+    def _(t):
+        pl.semaphore_signal(barrier, inc=1, device_id=(in_column(t),), device_id_type=MESH)
+
+    def cells_from(dst, tile_of, count):
+        for t in range(SUB):
+            v = pad_lanes(tile_of(t), LANES) if t < LT else jnp.zeros((count, LANES), F32)
+            dst[pl.ds(t, count, stride=SUB), :] = v
+
+    cells_from(m.kc, lambda t: kernel_ref[:, lanes(t)], TAPS)
+    for t in range(SUB):
+        for row, ref in ((0, gain_ref), (1, shift_ref)):
+            v = pad_lanes(ref[lanes(t)].reshape(1, -1), LANES) if t < LT else jnp.zeros((1, LANES), F32)
+            m.gc[row * SUB + t : row * SUB + t + 1, :] = v
+
+    loads[0].wait()
+    for copy in loads[1:]:
+        copy.start()
+    cells_from(m.xc, lambda t: m.x_nat[:, lanes(t)], CELLS)
+
+    def make_strips(src):
+        m.strip_top[...] = src[0 : EDGE * SUB, :].astype(BF)
+        m.strip_bot[...] = src[(CELLS - EDGE) * SUB : CELLS * SUB, :].astype(BF)
+        lef, rig = [], []
+        for r in range(TILE_SIDE):
+            row = r * TILE_SIDE * SUB
+            lef.append(src[row : row + MARGIN * SUB, :])
+            rig.append(src[row + (TILE_SIDE - MARGIN) * SUB : row + TILE_SIDE * SUB, :])
+        m.strip_lef[...] = jnp.concatenate(lef, axis=0).astype(BF)
+        m.strip_rig[...] = jnp.concatenate(rig, axis=0).astype(BF)
+
+    class Way:
+        def __init__(self, e, up):
+            self.e, self.up = e, up
+            self.sign = 1 if up else -1
+            self.strip = m.strip_bot if up else m.strip_top
+            self.buf = m.from_low if up else m.from_high
+            self.far_core = 1 if up else 0
+            self.near_core = 0 if up else 1
+            self.w = 0 if up else 1
+
+        def copy(self, src, slot, send, dev):
+            return remote(
+                src, self.buf.at[self.e, slot], m.halo_send.at[self.e, self.w, send], m.halo_recv.at[self.e, self.w, slot], dev
+            )
+
+        def to_there(self, k):
+            return (chip + k < s.chips) if self.up else (chip - k >= 0)
+
+        def from_there(self, k):
+            return (chip - k >= 0) if self.up else (chip + k < s.chips)
+
+        def direct(self, k):
+            return self.copy(self.strip, 2 * k, k, me + self.sign * 2 * k)
+
+        def far(self):
+            return self.copy(self.strip, REACH, 4, me + self.sign * REACH)
+
+        def near(self):
+            return self.copy(self.strip, 1, 5, twin)
+
+        def slot_at(self, k, its_core):
+            return 2 * k - 1 + 2 * its_core if self.up else 2 * k + 1 - 2 * its_core
+
+        def hand(self, k):
+            return self.copy(self.buf.at[self.e, 2 * k], self.slot_at(k, 1 - core), 5 + k, twin)
+
+        def handed(self, k):
+            return self.copy(self.strip, self.slot_at(k, core), 5 + k, twin)
+
+        def start(self):
+            for k in (3, 2, 1):
+
+                @pl.when(self.to_there(k))
+                def _(k=k):
+                    self.direct(k).start()
+
+            @pl.when(self.to_there(4) & (core == self.far_core))
+            def _():
+                self.far().start()
+
+            @pl.when(core == self.near_core)
+            def _():
+                self.near().start()
+
+        def relay(self):
+            for k in (1, 2, 3):
+
+                @pl.when(self.from_there(k))
+                def _(k=k):
+                    self.direct(k).wait_recv()
+                    self.hand(k).start()
+
+        def finish(self):
+            for k in (1, 2, 3):
+
+                @pl.when(self.from_there(k))
+                def _(k=k):
+                    self.hand(k).wait_send()
+                    self.handed(k).wait_recv()
+
+                @pl.when(self.to_there(k))
+                def _(k=k):
+                    self.direct(k).wait_send()
+
+            @pl.when(self.to_there(4) & (core == self.far_core))
+            def _():
+                self.far().wait_send()
+
+            @pl.when(self.from_there(4) & (core != self.far_core))
+            def _():
+                self.far().wait_recv()
+
+            @pl.when(core == self.near_core)
+            def _():
+                self.near().wait_send()
+
+            @pl.when(core != self.near_core)
+            def _():
+                self.near().wait_recv()
+
+    def east(e):
+        return remote(m.strip_rig, m.from_w.at[e, 1], m.side_send.at[e, 0], m.side_recv.at[e, 0], me + 1)
+
+    def west(e):
+        return remote(m.strip_lef, m.from_e.at[e, 1], m.side_send.at[e, 1], m.side_recv.at[e, 1], me - 1)
+
+    def halo_start(e):
+        Way(e, True).start()
+        Way(e, False).start()
+
+        @pl.when(me + 1 < N)
+        def _():
+            east(e).start()
+
+        @pl.when(me >= 1)
+        def _():
+            west(e).start()
+
+    def halo_relay(e):
+        Way(e, True).relay()
+        Way(e, False).relay()
+
+    def halo_finish(e):
+        Way(e, True).finish()
+        Way(e, False).finish()
+
+        @pl.when(me + 1 < N)
+        def _():
+            east(e).wait_send()
+            west(e).wait_recv()
+
+        @pl.when(me >= 1)
+        def _():
+            west(e).wait_send()
+            east(e).wait_recv()
+
+    zero_strip = jnp.zeros((EDGE * SUB, LANES), BF)
+    for e in range(2):
+        m.from_low[e, 0] = zero_strip
+        m.from_high[e, 0] = zero_strip
+        m.from_w[e, 0] = zero_strip
+        m.from_e[e, 0] = zero_strip
+
+    def fill_pad(e, centre):
+        def low_slot(d):
+            n = nbr_ref[0, d]
+            return jnp.clip(jnp.where(n < 0, 0, me - lax.shift_right_arithmetic(n, 1)), 0, REACH)
+
+        def high_slot(d):
+            n = nbr_ref[0, d]
+            return jnp.clip(jnp.where(n < 0, 0, lax.shift_right_arithmetic(n, 1) - me), 0, REACH)
+
+        def there(d):
+            return jnp.where(nbr_ref[0, d] < 0, 0, 1)
+
+        def put(row, col, value):
+            at = (row * PAD_SIDE + col) * SUB
+            m.pad[at : at + value.shape[0], :] = value
+
+        S, M, T = SUB, MARGIN, TILE_SIDE
+        for buf, slot, dirs, row0 in ((m.from_low, low_slot, (0, 1, 2), 0), (m.from_high, high_slot, (5, 6, 7), M + T)):
+            left = buf[e, slot(dirs[0])].astype(F32)
+            mid = buf[e, slot(dirs[1])].astype(F32)
+            right = buf[e, slot(dirs[2])].astype(F32)
+            for r in range(M):
+                at = r * T * S
+                put(row0 + r, 0, left[at + (T - M) * S : at + T * S])
+                put(row0 + r, M, mid[at : at + T * S])
+                put(row0 + r, M + T, right[at : at + M * S])
+        from_west = m.from_w[e, there(3)].astype(F32)
+        from_east = m.from_e[e, there(4)].astype(F32)
+        for r in range(T):
+            put(M + r, 0, from_west[r * M * S : (r + 1) * M * S])
+            put(M + r, M, centre[r * T * S : (r + 1) * T * S, :])
+            put(M + r, M + T, from_east[r * M * S : (r + 1) * M * S])
+
+    make_strips(m.xc)
+    n_partners = jnp.minimum(REACH, N - 1 - me) + jnp.minimum(REACH, me) + (Q - 1)
+    pl.semaphore_wait(barrier, n_partners)
+    halo_start(0)
+
+    eye = lax.broadcasted_iota(jnp.int32, (CELLS, CELLS), 0) == lax.broadcasted_iota(jnp.int32, (CELLS, CELLS), 1)
+    mask_row = maskv_ref[0:1, :].astype(F32)
+    mask_col = jnp.sum(jnp.where(eye, mask_row, 0.0), axis=1, keepdims=True)
+    n_mine = jnp.sum(mask_row)
+    loads[1].wait()
+    m.ups[...] = (m.cot_nat[...] * mask_col).astype(BF)
+    across_x = j + 1 - 2 * lax.rem(j, 2)
+    across_y = lax.rem(j + 2, CHIPS)
+    across = CHIPS - 1 - j
+    dev_x = q * INNER + 2 * across_x + core
+    dev_y = q * INNER + 2 * across_y + core
+    part_a = (0, 5 * 16)
+    part_b = (5 * 16, CELLS)
+    every = (0, CELLS)
+
+    class Rows:
+        def __init__(self, which, src, dst):
+            self.which, self.src, self.dst = which, src, dst
+
+        def at(self, jj, cc, part):
+            return self.dst.at[cc, pl.ds(pl.multiple_of(jj * CELLS + part[0], 16), part[1] - part[0])]
+
+        def copy(self, sem, src, jj, cc, part, dev):
+            return remote(src, self.at(jj, cc, part), m.rows_send.at[self.which, sem], m.rows_recv.at[self.which, sem], dev)
+
+        def sends(self):
+            own = [(0, self.src, j, every, dev_x), (1, self.src, j, every, dev_y), (4, self.src, j, every, twin)]
+            for sem, jj, part, dev in (
+                (2, across_x, part_a, dev_y),
+                (3, across_y, part_b, dev_x),
+                (5, across_x, every, twin),
+                (6, across_y, every, twin),
+                (7, across, part_a, twin),
+                (8, across, part_b, twin),
+            ):
+                own.append((sem, self.at(jj, core, part), jj, part, dev))
+            return {o[0]: functools.partial(self.copy, o[0], o[1], o[2], core, o[3], o[4]) for o in own}
+
+        def arrivals(self):
+            return {
+                sem: functools.partial(self.copy, sem, self.at(jj, cc, part), jj, cc, part, twin)
+                for sem, jj, cc, part in (
+                    (0, across_x, core, every),
+                    (1, across_y, core, every),
+                    (2, across, core, part_a),
+                    (3, across, core, part_b),
+                    (4, j, 1 - core, every),
+                    (5, across_x, 1 - core, every),
+                    (6, across_y, 1 - core, every),
+                    (7, across, 1 - core, part_a),
+                    (8, across, 1 - core, part_b),
+                )
+            }
+
+        def start(self):
+            for sem in (0, 1, 4):
+                self.sends()[sem]().start()
+            self.dst[core, pl.ds(pl.multiple_of(j * CELLS, 16), CELLS), :] = self.src[...]
+
+        def relay(self):
+            for came, then in ((0, (2, 5)), (1, (3, 6))):
+                self.arrivals()[came]().wait_recv()
+                for sem in then:
+                    self.sends()[sem]().start()
+
+        def relay_across(self):
+            for came, then in ((2, 7), (3, 8)):
+                self.arrivals()[came]().wait_recv()
+                self.sends()[then]().start()
+
+        def finish(self):
+            for sem in range(4, 9):
+                self.arrivals()[sem]().wait_recv()
+            for sem in range(9):
+                self.sends()[sem]().wait_send()
+
+    ups_rows = Rows(0, m.ups, m.uall)
+    dev_rows = Rows(1, m.dev, m.nall)
+    halo_relay(0)
+    ups_rows.start()
+    halo_finish(0)
+    fill_pad(0, m.xc)
+
+    def depthwise(dst, flip):
+        @pl.loop(0, TILE_SIDE)
+        def _(r):
+            acc = [None] * TILE_SIDE
+            for a in range(KERNEL):
+                base = pl.multiple_of((r + a) * (PAD_SIDE * SUB), SUB)
+                row = [m.pad[pl.ds(base + i * SUB, SUB), :] for i in range(PAD_SIDE)]
+                for b in range(KERNEL):
+                    tap = a * KERNEL + b
+                    if flip:
+                        tap = TAPS - 1 - tap
+                    k = m.kc[tap * SUB : (tap + 1) * SUB, :]
+                    for c in range(TILE_SIDE):
+                        term = k * row[c + b]
+                        acc[c] = term if acc[c] is None else acc[c] + term
+            out = pl.multiple_of(r * (TILE_SIDE * SUB), SUB)
+            for c in range(TILE_SIDE):
+                dst[pl.ds(out + c * SUB, SUB), :] = acc[c]
+
+    depthwise(m.conv, False)
+
+    def cell_mask(i):
+        return mask_ref[0, i].astype(F32)
+
+    def over_cells(fun, init):
+        def body(r, carry):
+            at = r * TILE_SIDE
+            for c in range(TILE_SIDE):
+                rows = pl.ds(pl.multiple_of(at * SUB, SUB) + c * SUB, SUB)
+                carry = fun(at + c, rows, carry)
+            return carry
+
+        return lax.fori_loop(0, TILE_SIDE, body, init)
+
+    zero = jnp.zeros((SUB, LANES), F32)
+    my_sum = over_cells(lambda i, rows, acc: acc + m.conv[rows, :] * cell_mask(i), zero)
+    my_mean = my_sum / n_mine
+
+    def deviation(i, rows, acc):
+        d = m.conv[rows, :] - my_mean
+        return acc + d * d * cell_mask(i)
+
+    my_dev = over_cells(deviation, zero)
+    sub_row = lax.broadcasted_iota(jnp.int32, (SUB, LANES), 0)
+
+    def put_moments(ref, total, dev, count):
+        ref[0:SUB, :] = jnp.where(sub_row == SUB - 1, count, total)
+        ref[SUB : 2 * SUB, :] = dev
+
+    def run(lo, hi, copy):
+        @pl.loop(lo, hi)
+        def _(k):
+            copy(k).start()
+
+        @pl.loop(lo, hi)
+        def _(k):
+            copy(k).wait()
+
+    class Spread:
+        def __init__(self, src, slots, send, recv, count, dev):
+            self.src, self.slots, self.send, self.recv, self.count, self.dev = src, slots, send, recv, count, dev
+
+        def start(self):
+            for k in range(1, self.count):
+                remote(self.src, self.slots.at[k], self.send, self.recv, self.dev(k)).start()
+
+        def finish(self):
+            whole = self.slots.at[1 : self.count]
+            copy = remote(whole, whole, self.send, self.recv, twin)
+            copy.wait_send()
+            copy.wait_recv()
+
+    def in_planes(e):
+        return Spread(m.stat_sa.at[e], m.stat_a.at[e], m.vec_send.at[e], m.vec_recv.at[e], INNER, in_plane)
+
+    def in_columns(e):
+        return Spread(m.stat_sb.at[e], m.stat_b.at[e], m.col_send.at[e], m.col_recv.at[e], Q, in_column)
+
+    def merge_moments(msgs):
+        counts = [v[SUB - 1 : SUB, :] for v in msgs]
+        total, n = msgs[0][0:SUB], counts[0]
+        for v, c in zip(msgs[1:], counts[1:]):
+            total, n = total + v[0:SUB], n + c
+        mean = total / n
+        dev = zero
+        for v, c in zip(msgs, counts):
+            off = v[0:SUB] / c - mean
+            dev = dev + v[SUB : 2 * SUB] + c * off * off
+        return total, dev, n, mean
+
+    put_moments(m.stat_sa.at[0], my_sum, my_dev, n_mine)
+    in_planes(0).start()
+    for t in range(LT):
+        v = m.conv[pl.ds(t, CELLS, stride=SUB), :] - my_mean[t : t + 1]
+        m.dev[:, lanes(t)] = (v[:, :tail] if t == LT - 1 else v).astype(BF)
+    dev_rows.start()
+
+    loads[2].wait()
+    chunk = 5 * LANES
+
+    @pl.loop(0, H // chunk)
+    def _(i):
+        cols = pl.ds(pl.multiple_of(i * chunk, chunk), chunk)
+        m.actg[:, cols] = dot(m.ups[...], m.wout[:, cols])
+
+    in_planes(0).finish()
+    plane_sum, plane_dev, plane_n, _ = merge_moments([m.stat_sa[0]] + [m.stat_a[0, k] for k in range(1, INNER)])
+    put_moments(m.stat_sb.at[0], plane_sum, plane_dev, plane_n)
+    in_columns(0).start()
+    ups_rows.relay()
+    loads[3].wait()
+    width = min(2 * LANES, H)
+    for weight, dst in ((m.win, m.wi_t), (m.wout, m.wo_t)):
+        for b in range(Q):
+            start = b * (H // Q) + p * hb
+            first = pl.multiple_of(jnp.minimum((start // LANES) * LANES, H - width), LANES)
+            pick_row = lax.broadcasted_iota(jnp.int32, (LANES, width), 0)
+            pick_col = lax.broadcasted_iota(jnp.int32, (LANES, width), 1)
+            pick = ((pick_col == pick_row + (start - first)) & (pick_row < hb)).astype(F32)
+            m.big[b * hb : b * hb + LANES, :] = dot(pick.astype(BF), weight[:, pl.ds(first, width)], NT)
+            if dst is m.wi_t:
+                row = bin_ref[pl.ds(first, width)].reshape(1, width)
+                m.bi_t[b * hb : b * hb + LANES, :] = jnp.sum(pick * row, axis=1, keepdims=True)
+        dst[...] = m.big[0:hq, :].astype(BF)
+
+    in_columns(0).finish()
+    _, all_dev, n_row, mean = merge_moments([m.stat_sb[0]] + [m.stat_b[0, t] for t in range(1, Q)])
+    inv = lax.rsqrt(all_dev / n_row + EPSILON)
+    gain_c = m.gc[0:SUB, :]
+    shift_c = m.gc[SUB : 2 * SUB, :]
+    scale_c = inv * gain_c
+    inv_n = 1.0 / n_row
+
+    for t in range(LT):
+        v = m.conv[pl.ds(t, CELLS, stride=SUB), :]
+        v = (v - mean[t : t + 1]) * inv[t : t + 1] * gain_c[t : t + 1] + shift_c[t : t + 1]
+        m.nrm[:, lanes(t)] = (v[:, :tail] if t == LT - 1 else v).astype(BF)
+
+    m.kg[...] = jnp.zeros_like(m.kg)
+    m.branch[...] = jnp.zeros_like(m.branch)
+    m.ng[...] = jnp.zeros_like(m.ng)
+
+    def pointwise(i, _):
+        at = pl.multiple_of(i * chunk, chunk)
+        cols = pl.ds(at, chunk)
+        pre = dot(m.nrm[...], m.win[:, cols]) + bin_ref[cols].reshape(1, chunk)
+        act, slope = gelu_parts(pre)
+        pg = (m.actg[:, cols] * slope).astype(BF)
+        m.branch[...] += dot(act.astype(BF), m.wout[:, cols], NT)
+        m.ng[...] += dot(pg, m.win[:, cols], NT)
+        bias = jnp.sum(pg.astype(F32), axis=0, keepdims=True)
+        for k in range(chunk // LANES):
+            m.kg[pl.ds(TAPS * SUB + i * (chunk // LANES) + k, 1), :] = bias[:, k * LANES : (k + 1) * LANES]
+        return 0
+
+    half_way = H // chunk // 2
+    lax.fori_loop(0, half_way, pointwise, 0)
+    ups_rows.relay_across()
+    dev_rows.relay()
+    lax.fori_loop(half_way, H // chunk, pointwise, 0)
+
+    cells_from(m.ngc, lambda t: m.ng[:, lanes(t)], CELLS)
+
+    def grads(i, rows, carry):
+        g = m.ngc[rows, :]
+        return carry[0] + g, carry[1] + g * ((m.conv[rows, :] - mean) * inv)
+
+    shift_part, gain_part = over_cells(grads, (zero, zero))
+    m.stat_sa[1, 0:SUB, :] = shift_part
+    m.stat_sa[1, SUB : 2 * SUB, :] = gain_part
+    in_planes(1).start()
+    dev_rows.relay_across()
+    m.branch[...] = (m.x_nat[...] + m.branch[...] + bout_ref[...].reshape(1, C)) * mask_col
+    out_block = pltpu.make_async_copy(m.branch, o_block, m.out_sem.at[0])
+    out_block.start()
+    bias = jnp.sum(m.ups[...].astype(F32), axis=0, keepdims=True)
+    for t in range(LT):
+        at = TAPS * SUB + s.bias_rows + t
+        m.kg[at : at + 1, :] = pad_lanes(bias[:, lanes(t)], LANES)
+
+    in_planes(1).finish()
+    tot = m.stat_sa[1]
+    for k in range(1, INNER):
+        tot = tot + m.stat_a[1, k]
+    m.stat_sb[1] = tot
+    in_columns(1).start()
+    ups_rows.finish()
+    dev_rows.finish()
+    for k in range(1, INNER):
+        pk = lax.rem(p + INNER - k, INNER)
+        rows = pl.ds(pl.multiple_of((pk // 2) * CELLS, 16), CELLS)
+        cc = lax.rem(pk, 2)
+        its = m.stat_a[0, k]
+        off = (its[0:SUB] / its[SUB - 1 : SUB] - mean) * scale_c + shift_c
+        for t in range(LT):
+            w = lanes(t).stop - lanes(t).start
+            v = m.nall[cc, rows, lanes(t)].astype(F32)
+            m.nall[cc, rows, lanes(t)] = (v * scale_c[t : t + 1, :w] + off[t : t + 1, :w]).astype(BF)
+    m.nall[core, pl.ds(pl.multiple_of(j * CELLS, 16), CELLS), :] = m.nrm[...]
+    for cc in (core, 1 - core):
+        for lo, hi in ((0, 2 * LANES), (2 * LANES, s.half_rows)):
+            pre = dot(m.wi_t[...], m.nall[cc, lo:hi, :], NT) + m.bi_t[0:hq, :]
+            act, slope = gelu_parts(pre)
+            m.act_t[cc, :, lo:hi] = act.astype(BF)
+            m.pg_t[cc, :, lo:hi] = (dot(m.wo_t[...], m.uall[cc, lo:hi, :], NT) * slope).astype(BF)
+
+    def keep_rows(value, rows):
+        for t in range(-(-value.shape[1] // LANES)):
+            m.tiles[t * rows : (t + 1) * rows, :] = pad_lanes(value[:, t * LANES : (t + 1) * LANES], LANES)
+
+    def lay_out(rows, count, width, dst):
+        long = count * width // SUB
+        tiles = -(-width // LANES)
+        groups = {}
+        for r in range(SUB):
+            groups.setdefault(r * long % width, []).append(r)
+        for off, rs in groups.items():
+            first = [r * long // width for r in rs]
+            n = len(rs)
+            step = first[1] - first[0] if n > 1 else 1
+            assert all(f == first[0] + i * step for i, f in enumerate(first))
+            pieces, row, at, left = [], first[0], off, long
+            while left:
+                w = min(left, width - at)
+                for t in range(at // LANES, -(-(at + w) // LANES)):
+                    lo, hi = max(at, t * LANES), min(at + w, (t + 1) * LANES)
+                    where = pl.ds(t * rows + row, n, stride=step) if n > 1 else pl.ds(t * rows + row, 1)
+                    pieces.append(m.tiles[where, :][:, lo - t * LANES : hi - t * LANES])
+                row, at, left = row + 1, 0, left - w
+            v = jnp.concatenate(pieces, axis=1)
+            for t in range(-(-long // LANES)):
+                w = min(LANES, long - t * LANES)
+                where = pl.ds(t * SUB + rs[0], n, stride=rs[1] - rs[0]) if n > 1 else pl.ds(t * SUB + rs[0], 1)
+                m.long[where, :] = pad_lanes(v[:, t * LANES : t * LANES + w], LANES)
+        for t in range(-(-long // LANES)):
+            w = min(LANES, long - t * LANES)
+            dst[:, t * LANES : t * LANES + w] = m.long[t * SUB : (t + 1) * SUB, :][:, :w]
+
+    in_columns(1).finish()
+    for t in range(1, Q):
+        tot = tot + m.stat_b[1, t]
+    shift_grad, gain_grad = tot[0:SUB], tot[SUB : 2 * SUB]
+
+    def to_conv_grad(r, _):
+        at = r * TILE_SIDE
+        for c in range(TILE_SIDE):
+            rows = pl.ds(pl.multiple_of(at * SUB, SUB) + c * SUB, SUB)
+            scaled = (m.conv[rows, :] - mean) * inv
+            m.ngc[rows, :] = scale_c * (
+                m.ngc[rows, :] - cell_mask(at + c) * (shift_grad + scaled * gain_grad) * inv_n
+            )
+        return 0
+
+    lax.fori_loop(0, TILE_SIDE, to_conv_grad, 0)
+    make_strips(m.ngc)
+    halo_start(1)
+
+    nb, pr, width_in = s.blocks, s.pack_rows, s.blocks * cq
+
+    def pack_in(b):
+        cols = slice(b * cq, (b + 1) * cq)
+        return pad_lanes(jnp.concatenate([m.big[i * pr : (i + 1) * pr, cols] for i in range(nb)], axis=1), s.pack_lanes)
+
+    def pack_out(b):
+        top = m.big[b * hb : b * hb + pr, :]
+        rest = m.big[b * hb + pr : (b + 1) * hb, :]
+        side = jnp.concatenate([rest[:, g * cq : (g + 1) * cq] for g in range(Q)], axis=0)
+        return pad_lanes(jnp.concatenate([top, side], axis=1), s.pack_lanes)
+
+    def z_up(kind, b):
+        return remote(m.zsrc.at[kind, b], m.zup.at[kind, b], m.z_send.at[kind, b], m.z_up.at[kind, b], me + INNER)
+
+    def z_dn(kind, b):
+        return remote(m.zsrc.at[kind, b], m.zdn.at[kind, b], m.z_send.at[kind, b], m.z_dn.at[kind, b], me - INNER)
+
+    def z_add(kind, b, buf):
+        m.zsrc[kind, b] = (m.zsrc[kind, b].astype(F32) + buf[kind, b].astype(F32)).astype(BF)
+
+    def z_hop(kind, hop):
+        @pl.when(q == hop)
+        def _():
+            for b in range(Q - 1, hop, -1):
+                if hop > 0:
+                    z_up(kind, b).wait_recv()
+                    z_add(kind, b, m.zup)
+                z_up(kind, b).start()
+
+        @pl.when(q == Q - 1 - hop)
+        def _():
+            for b in range(0, Q - 1 - hop):
+                if hop > 0:
+                    z_dn(kind, b).wait_recv()
+                    z_add(kind, b, m.zdn)
+                z_dn(kind, b).start()
+
+    def z_total(kind):
+        for b in range(Q):
+
+            @pl.when(q > b)
+            def _(b=b):
+                z_dn(kind, b).wait_send()
+
+            @pl.when(q < b)
+            def _(b=b):
+                z_up(kind, b).wait_send()
+
+        @pl.when(q > 0)
+        def _():
+            z_up(kind, q).wait_recv()
+
+        @pl.when(q < Q - 1)
+        def _():
+            z_dn(kind, q).wait_recv()
+
+        low = jnp.where(q > 0, m.zup[kind, q].astype(F32), 0.0)
+        high = jnp.where(q < Q - 1, m.zdn[kind, q].astype(F32), 0.0)
+        return m.zown[kind] + low + high
+
+    def keep_packed(kind, pack):
+        for b in range(Q):
+            v = pack(b)
+            m.zsrc[kind, b] = v.astype(BF)
+
+            @pl.when(q == b)
+            def _(v=v):
+                m.zown[kind] = v
+
+    def product(a, rows):
+        m.big[0:hq, :] = dot(a[0], rows[0]) + dot(a[1], rows[1])
+
+    product(m.pg_t, m.nall)
+    keep_packed(0, pack_in)
+    z_hop(0, 0)
+    product(m.act_t, m.uall)
+    keep_packed(1, pack_out)
+    z_hop(1, 0)
+    @pl.loop(0, KERNEL)
+    def _(a):
+        acc = [zero] * KERNEL
+        for r in range(TILE_SIDE):
+            base = pl.multiple_of((r + a) * (PAD_SIDE * SUB), SUB)
+            row = [m.pad[pl.ds(base + i * SUB, SUB), :] for i in range(PAD_SIDE)]
+            for c in range(TILE_SIDE):
+                g = m.ngc[(r * TILE_SIDE + c) * SUB : (r * TILE_SIDE + c + 1) * SUB, :]
+                for b in range(KERNEL):
+                    acc[b] = acc[b] + g * row[c + b]
+        for b in range(KERNEL):
+            m.kg[pl.ds(pl.multiple_of(a * (KERNEL * SUB), SUB) + b * SUB, SUB), :] = acc[b]
+
+    part = s.kg_rows // INNER
+    mine = pl.ds(pl.multiple_of(p * part, SUB), part)
+
+    def part_of(k):
+        return pl.ds(pl.multiple_of(k * part, SUB), part)
+
+    for k in range(1, INNER):
+        remote(m.kg.at[part_of(lax.rem(p + k, INNER))], m.kg_slot.at[k], m.ks_send.at[0], m.ks_recv.at[0], in_plane(k)).start()
+
+    column_sum = Spread(m.kg_col.at[0], m.kg_col, m.ks_send.at[1], m.ks_recv.at[1], Q, in_column)
+
+    z_hop(0, 1)
+    halo_relay(1)
+    halo_finish(1)
+    fill_pad(1, m.ngc)
+    depthwise(m.conv, True)
+    for t in range(LT):
+        v = m.conv[pl.ds(t, CELLS, stride=SUB), :]
+        m.ng[:, lanes(t)] = v[:, :tail] if t == LT - 1 else v
+    m.ng[...] += m.cot_nat[...] * mask_col
+    out_fgrad = pltpu.make_async_copy(m.ng, o_fgrad, m.out_sem.at[1])
+    out_fgrad.start()
+
+    whole = m.kg_slot.at[1:INNER]
+    copy = remote(whole, whole, m.ks_send.at[0], m.ks_recv.at[0], twin)
+    copy.wait_send()
+    copy.wait_recv()
+    part_sum = m.kg[mine, :]
+    for k in range(1, INNER):
+        part_sum = part_sum + m.kg_slot[k]
+    m.kg_col[0] = part_sum
+    column_sum.start()
+    for hop in range(2, Q - 1):
+        z_hop(0, hop)
+    column_sum.finish()
+    for t in range(1, Q):
+        part_sum = part_sum + m.kg_col[t]
+    m.kg_tot[p] = part_sum
+    for k in range(1, INNER):
+        remote(m.kg_tot.at[p], m.kg_tot.at[p], m.ks_send.at[2], m.ks_recv.at[2], in_plane(k)).start()
+
+    total = z_total(0)
+    flat = jnp.concatenate([total[:, i * cq : (i + 1) * cq] for i in range(nb)], axis=0)
+    flat = jnp.concatenate([flat, jnp.zeros((s.tr_lanes - hq, cq), F32)], axis=0)
+    m.tr[...] = pad_lanes(flat, 2 * LANES).T
+    for d in range(INNER):
+        m.tr_src[d] = m.tr[d * cb : d * cb + s.in_rows, :]
+
+    for k in range(1, INNER):
+        remote(m.tr_src.at[lax.rem(p + k, INNER)], m.tr_dst.at[p], m.tr_send.at[0], m.tr_recv.at[0], in_plane(k)).start()
+    m.tr_dst[p] = m.tr_src[p]
+    z_hop(1, 1)
+
+    whole = m.kg_tot.at[1:INNER]
+    copy = remote(whole, whole, m.ks_send.at[2], m.ks_recv.at[2], twin)
+    copy.wait_send()
+    copy.wait_recv()
+
+    m.kg[...] = jnp.concatenate([m.kg_tot[k] for k in range(INNER)], axis=0)
+    for t in range(LT):
+        v = m.kg[pl.ds(t, TAPS, stride=SUB), :]
+        o_kgrad[:, lanes(t)] = v[:, :tail] if t == LT - 1 else v
+
+    def to_vector(ref, row, length):
+        for t in range(-(-length // LANES)):
+            w = min(LANES, length - t * LANES)
+            ref[t * LANES : t * LANES + w] = m.kg[row + t, :][:w]
+
+    to_vector(o_bin, TAPS * SUB, H)
+    to_vector(o_bout, TAPS * SUB + s.bias_rows, C)
+    m.kg[0:SUB, :] = shift_grad
+    m.kg[SUB : 2 * SUB, :] = gain_grad
+    to_vector(o_shift, 0, C)
+    to_vector(o_gain, SUB, C)
+
+    copy = remote(m.tr_dst.at[1:INNER], m.tr_dst.at[1:INNER], m.tr_send.at[0], m.tr_recv.at[0], twin)
+    copy.wait_send()
+    copy.wait_recv()
+    pieces = []
+    for b in range(Q):
+        for d in range(INNER):
+            pieces.append(m.tr_dst[d][:, b * hb : (b + 1) * hb])
+    keep_rows(jnp.concatenate(pieces, axis=1)[: s.in_rows], s.in_rows)
+    lay_out(s.in_rows, cb, H, o_win)
+    for hop in range(2, Q - 1):
+        z_hop(1, hop)
+
+    total = z_total(1)
+    side = total[:, C:width_in]
+    rest = hb - pr
+    side = jnp.concatenate([side[g * rest : (g + 1) * rest] for g in range(Q)], axis=1)
+    spare = jnp.zeros((s.out_rows - hb, C), F32)
+    keep_rows(jnp.concatenate([total[:, :C], side, spare], axis=0), s.out_rows)
+    lay_out(s.out_rows, hb, C, o_wout)
+    out_block.wait()
+    out_fgrad.wait()
+
+
+def run_step(s, fields, cotangent, kernel, norm_gain, norm_shift, weight_in, bias_in, weight_out, bias_out, neighbours, land_mask):
+    C, H = s.C, s.H
+    any_ = pl.BlockSpec(memory_space=pl.ANY)
+    vmem = pl.BlockSpec(memory_space=pltpu.VMEM)
+    smem = pl.BlockSpec(memory_space=pltpu.SMEM)
+    long = (SUB, C * H // (SUB * s.N))
+    shapes = ((CELLS, C), (CELLS, C), (TAPS, C), (C,), (C,), long, (H,), long, (C,))
+    outs = [jax.ShapeDtypeStruct(shape, F32) for shape in shapes]
+    scratch = scratch_of(s)
+    return pl.pallas_call(
+        functools.partial(step_kernel, s, tuple(scratch)),
+        out_shape=outs,
+        in_specs=[any_, any_, vmem, vmem, vmem, any_, vmem, any_, vmem, smem, smem, vmem],
+        out_specs=[any_, any_] + [vmem] * 7,
+        scratch_shapes=list(scratch.values()),
+        compiler_params=pltpu.CompilerParams(
+            collective_id=0, has_side_effects=True, vmem_limit_bytes=58 * 1024 * 1024
+        ),
+        cost_estimate=pl.CostEstimate(
+            flops=20 * CELLS * C * H, bytes_accessed=4 * C * H + 8 * CELLS * C, transcendentals=4 * CELLS * H
+        ),
+        name="step",
+    )(
+        fields,
+        cotangent,
+        kernel,
+        norm_gain,
+        norm_shift,
+        weight_in,
+        bias_in,
+        weight_out.T,
+        bias_out,
+        neighbours,
+        land_mask,
+        land_mask,
+    )
+
+
+def finish_kernel(count, *refs):
+    ins, outs, zeros = refs[:count], refs[count : 2 * count], refs[2 * count]
+    held, sems, out_sems = refs[2 * count + 1 : 3 * count + 1], refs[3 * count + 1], refs[3 * count + 2]
+    into = [pltpu.make_async_copy(src, dst, sems.at[i]) for i, (src, dst) in enumerate(zip(ins, held))]
+    for copy in into:
+        copy.start()
+    zeros[...] = jnp.zeros_like(zeros)
+    out = [pltpu.make_async_copy(zeros, outs[i].at[1], out_sems.at[count + i]) for i in range(2)]
+    for copy in out:
+        copy.start()
+    for i in range(count):
+        into[i].wait()
+        out.append(pltpu.make_async_copy(held[i], outs[i].at[0] if i < 2 else outs[i], out_sems.at[i]))
+        out[-1].start()
+    for copy in out:
+        copy.wait()
+
+
+def local_step(s, fields, *rest):
+    parts = run_step(s, fields, *rest)
+    count = len(parts)
+    any_ = pl.BlockSpec(memory_space=pl.ANY)
+    outs = [jax.ShapeDtypeStruct(fields.shape if i < 2 else v.shape, F32) for i, v in enumerate(parts)]
+    held = [pltpu.VMEM(v.shape, F32) for v in parts]
+    return tuple(
+        pl.pallas_call(
+            functools.partial(finish_kernel, count),
+            out_shape=outs,
+            in_specs=[any_] * count,
+            out_specs=[any_] * count,
+            scratch_shapes=[pltpu.VMEM((CELLS, s.C), F32)]
+            + held
+            + [pltpu.SemaphoreType.DMA((count,)), pltpu.SemaphoreType.DMA((count + 2,))],
+            name="finish",
+        )(*parts)
+    )
 
 
 def from_behind(shard, axis, by):
@@ -92,7 +1106,7 @@
     )
 
 
-def local(
+def general(
     fields,
     cotangent,
     kernel,
@@ -181,33 +1195,43 @@
     )
 
 
+IN_SPECS = (
+    P("tile", None, None),
+    P("tile", None, None),
+    P(),
+    P(),
+    P(),
+    P(),
+    P(),
+    P(),
+    P(),
+    P("tile", None),
+    P("tile", None),
+)
+OUT_SPECS = (
+    P("tile", None, None),
+    P("tile", None, None),
+    P(),
+    P(),
+    P(),
+    P("tile", None),
+    P(),
+    P("tile", None),
+    P(),
+)
+
+
 def solution(mesh):
-    return jax.shard_map(
-        local,
-        mesh=mesh,
-        in_specs=(
-            P("tile", None, None),
-            P("tile", None, None),
-            P(),
-            P(),
-            P(),
-            P(),
-            P(),
-            P(),
-            P(),
-            P("tile", None),
-            P("tile", None),
-        ),
-        out_specs=(
-            P("tile", None, None),
-            P("tile", None, None),
-            P(),
-            P(),
-            P(),
-            P("tile", None),
-            P(),
-            P("tile", None),
-            P(),
-        ),
-        check_vma=False,
-    )
+    N = mesh.shape["tile"]
+
+    def whole(fields, cotangent, kernel, norm_gain, norm_shift, weight_in, *rest):
+        C, H = weight_in.shape
+        if Sizes.fits(N, C, H) and fields.shape[0] == 2 * N:
+            body = functools.partial(local_step, Sizes(N, C, H))
+        else:
+            body = general
+        return jax.shard_map(body, mesh=mesh, in_specs=IN_SPECS, out_specs=OUT_SPECS, check_vma=False)(
+            fields, cotangent, kernel, norm_gain, norm_shift, weight_in, *rest
+        )
+
+    return whole

time: 1190 us -> 92.9 us (0.08); the launches traced: 1180 us -> 92.6 us
  waiting for transfers between devices: 342 us -> 0 us
  other arithmetic: 202 us -> 0 us
  starting transfers between devices: 195 us -> 0 us
  local copies, waits for them, and re-layouts: 194 us -> 0 us
  blocking collectives: 180 us -> 0 us
  Pallas kernels: 0 us -> 91.9 us
  matrix products: 47.6 us -> 0 us
  between operations: 16.5 us -> 0.65 us
    psum x1 -> x0, waiting for transfers between devices: 227 us -> none  [local(): kernel_grad = lax.psum(kernel_part, 'tile')]
    ppermute x28 -> x0, starting transfers between devices: 195 us -> none  [from_behind(): return lax.ppermute(shard, axis, pairs)]
    psum x3 -> x0, blocking collectives: 180 us -> none  [the longest x1 98 us: local(): lax.psum((jnp.sum(ocean), jnp.sum(conv * cell_weight, axis=(0, 1))), 'tile')]
    ppermute x28 -> x0, waiting for transfers between devices: 115 us -> none  [from_behind(): return lax.ppermute(shard, axis, pairs)]
    pallas_call x0 -> x2, Pallas kernels: none -> 91.9 us  [the longest x1 89.1 us: run_step(): pl.pallas_call(functools.partial(step_kernel, s, tuple(scratch)), out_sha...]
    add_any x3 -> x0, other arithmetic: 82.6 us -> none  [the longest x1 75.2 us: depthwise(): padded[:, row_tap:row_tap + tile_side, col_tap:col_tap + tile_side]]
    reduce_sum x8 -> x0, other arithmetic: 80.3 us -> none  [the longest x4 40.5 us: depthwise(): kernel[row_tap * KERNEL + col_tap]]
    dot_general x7 -> x0, matrix products: 47.6 us -> none  [the longest x1 14.8 us: local(): jnp.dot(choose, nearby_grad.reshape(slots * 8, -1), precision=lax.Precisi...]
  transfers between devices with their start and end apart: 29 -> 0, of which waited for: 9 -> 0; matrix products, arithmetic and copies ran while one was open for 8% -> 0% of each run, Pallas kernels for 0% -> 0%
where the time goes in v2:
time: 92.9 us; the launch traced here: 92.6 us
  Pallas kernels  91.9 us (99%)
    pallas_call x1, Pallas kernels, run_step(): pl.pallas_call(functools.partial(step_kernel, s, tuple(scratch)), out_sha...  89.1 us
    pallas_call x1, Pallas kernels, local_step(): pl.pallas_call(functools.partial(finish_kernel, count), out_shape=outs, i...  2.83 us

profile of v2, /device:TPU:0, one launch (start us, length us, event | category | flops | bytes accessed | tf_op | source)
XLA Modules:
  0.0 92.6 jit_solution(12905375565587679815)
XLA Ops:
  0.6 89.1 %step.1 = (f32[144,800]{1,0:T(8,128)}, f32[144,800]{1,0:T(8,128)}, f32[49,800]{1,0:T(8,128)}, f32[800]{0:T(1024)}, f32[800]{0:T(1024)}, /*index=5*/f32[8,10000]{...) custom-call(f32[2,144,800]{2,1,0:T(8,128)} %refs_0_.1, f32[2,144,800]{2,1,0:T(8,128)} %refs_1_.1, ...), custom_call_target="tpu_custom_call" | custom-call | flops 7372800000 | bytes 11161600 | tf_op jit(solution)/shard_map/step/pallas_call | solution.py:964
  89.8 2.8 %finish.1 = (f32[2,144,800]{2,1,0:T(8,128)}, f32[2,144,800]{2,1,0:T(8,128)}, f32[49,800]{1,0:T(8,128)}, f32[800]{0:T(1024)}, f32[800]{0:T(1024)}, /*index=5*/f32...) custom-call(f32[144,800]{1,0:T(8,128)} %get-tuple-element.18.refs_0_, ...), custom_call_target="tpu_custom_call" | custom-call | tf_op jit(solution)/shard_map/finish/pallas_call | solution.py:1018
